TPU v7x, 512 devices: a whole 4x8x8 slice. The times are simulated.
512 devices in a mesh: tm: 16 (over y, core), head: 8 (over z), dp: 4 (over x).
Axes of the slice: x: 4, y: 8, z: 8, core: 2. Of those that a mesh axis runs over, the one named last changes fastest.
Arguments:
- frames: bfloat16 [4, 4096, 1280], P('dp', 'tm'), may hold values from -42 to 42
- masked: int32 [4, 4096], P('dp', 'tm'), may hold values from 0 to 1, as said below
- kept_counts: int32 [4, 16], P('dp', 'tm'), may hold values from 64 to 128, as said below
- teacher_qkv: bfloat16 [1280, 3, 1280], P('dp', None, 'head'), may hold values from -0.15625 to 0.15625
- student_gain: float32 [1280], replicated, may hold values from 0.1 to 1.9
- w_up: bfloat16 [1280, 5120], P('dp', 'head'), may hold values from -0.15625 to 0.15625
- w_down: bfloat16 [1280, 5120], P('dp', 'head'), may hold values from -0.078125 to 0.078125
Outputs:
- targets: bfloat16 [4, 4096, 1280], P('dp', 'tm', 'head')
- grad_up: float32 [1280, 5120], P('dp', 'head')
- grad_down: float32 [1280, 5120], P('dp', 'head')
Inputs may be any that keep to these rules, and one draw needn't show every extreme that they name: `masked`: shard t of a sequence keeps exactly kept_counts of its 256 frames. `kept_counts`: every sequence has a shard that keeps 128 frames, and its shards keep 1536 frames together.
All inputs are finite; a program needn't handle non-finite values.
Results may differ from a plain program's by a relative error of at most 0.02.
Values may be sent and summed in bfloat16 or wider, within the bound.
A program may use at most 64 MiB of HBM per device.

v0:
```python
import math

import jax
import jax.numpy as jnp
from jax import lax
from jax.sharding import PartitionSpec as P

D = 1280
HEAD_DIM = 80
CAP = 128


def gelu_exact(values):
    return jax.nn.gelu(values, approximate=False)


def local(frames, masked, kept_counts, teacher_qkv, student_gain, w_up, w_down):
    qkv_full, up_full, down_full = (
        lax.all_gather(teacher_qkv, "dp", axis=0, tiled=True),
        lax.all_gather(w_up, "dp", axis=0, tiled=True),
        lax.all_gather(w_down, "dp", axis=0, tiled=True),
    )
    sequence = frames[0]
    rows = sequence.shape[0]
    qkv = jnp.einsum("td,dke->tke", sequence, qkv_full, preferred_element_type=jnp.float32).astype(
        jnp.bfloat16
    )
    local_heads = qkv.shape[2] // HEAD_DIM
    query = qkv[:, 0].reshape(rows, local_heads, HEAD_DIM)
    paired = qkv[:, 1:3]
    scale = HEAD_DIM ** (-0.5)
    start_best = jnp.full((local_heads, rows), -jnp.inf, jnp.float32)
    start_total = jnp.zeros((local_heads, rows), jnp.float32)
    start_accum = jnp.zeros((local_heads, rows, HEAD_DIM), jnp.float32)
    piece = lax.all_gather(paired, "tm", axis=0, tiled=True)
    best = start_best
    total = start_total
    accum = start_accum
    keys = piece[:, 0].reshape(piece.shape[0], local_heads, HEAD_DIM)
    values = piece[:, 1].reshape(piece.shape[0], local_heads, HEAD_DIM)
    scores = jnp.einsum("thd,shd->hts", query, keys, preferred_element_type=jnp.float32) * scale
    new_best = jnp.max(scores, axis=2)
    fade = jnp.exp(best - new_best)
    weights = jnp.exp(scores - new_best[:, :, None])
    total = total * fade + jnp.sum(weights, axis=2)
    accum = accum * fade[:, :, None] + jnp.einsum(
        "hts,shd->htd", weights.astype(jnp.bfloat16), values, preferred_element_type=jnp.float32
    )
    best, total, accum = (new_best, total, accum)
    context = (accum / total[:, :, None]).transpose(1, 0, 2).reshape(rows, local_heads * HEAD_DIM)
    first_sum, second_sum = lax.psum(
        (jnp.sum(context, axis=0), jnp.sum(context * context, axis=0)), "tm"
    )
    length = rows * lax.axis_size("tm")
    mean = first_sum / length
    var = second_sum / length - mean * mean
    target = (context - mean) * lax.rsqrt(var + 1e-05)
    targets = target.astype(jnp.bfloat16)[None]
    keep = 1 - masked[0]
    index = jnp.nonzero(keep, size=CAP, fill_value=0)[0].astype(jnp.int32)
    valid = jnp.arange(CAP, dtype=jnp.int32) < kept_counts[0, 0]
    chosen = jnp.take(sequence, index, axis=0).astype(jnp.float32)
    centre = jnp.mean(chosen, axis=1, keepdims=True)
    spread = jnp.mean((chosen - centre) ** 2, axis=1, keepdims=True)
    normed = ((chosen - centre) * lax.rsqrt(spread + 1e-05) * student_gain).astype(jnp.bfloat16)
    pre = jnp.dot(normed, up_full, preferred_element_type=jnp.float32)
    act = gelu_exact(pre).astype(jnp.bfloat16)
    partial_pred = jnp.einsum("cf,df->cd", act, down_full, preferred_element_type=jnp.float32)
    aim = jnp.take(target, index, axis=0)
    factor = 2.0 / math.sqrt(D)
    whole_pred = lax.psum(partial_pred.astype(jnp.bfloat16), "head").astype(jnp.float32)
    whole_aim = lax.all_gather(aim.astype(jnp.bfloat16), "head", axis=1, tiled=True).astype(
        aim.dtype
    )
    cot = (jnp.where(valid[:, None], whole_pred - whole_aim, 0.0) * factor).astype(jnp.bfloat16)
    grad_down_term = jnp.einsum("cd,cf->df", cot, act, preferred_element_type=jnp.float32)
    d_act = jnp.dot(cot, down_full, preferred_element_type=jnp.float32)
    d_pre = jax.vjp(gelu_exact, pre)[1](d_act)[0].astype(jnp.bfloat16)
    grad_up_term = jnp.einsum("cd,cf->df", normed, d_pre, preferred_element_type=jnp.float32)
    slice_up, slice_down = (
        lax.psum_scatter(
            grad_up_term.astype(jnp.bfloat16), "tm", scatter_dimension=0, tiled=True
        ).astype(jnp.float32),
        lax.psum_scatter(
            grad_down_term.astype(jnp.bfloat16), "tm", scatter_dimension=0, tiled=True
        ).astype(jnp.float32),
    )
    batch_up, batch_down = (
        lax.psum(slice_up.astype(jnp.bfloat16), "dp").astype(jnp.float32),
        lax.psum(slice_down.astype(jnp.bfloat16), "dp").astype(jnp.float32),
    )
    whole_up, whole_down = (
        lax.all_gather(batch_up.astype(jnp.bfloat16), "tm", axis=0, tiled=True).astype(
            batch_up.dtype
        ),
        lax.all_gather(batch_down.astype(jnp.bfloat16), "tm", axis=0, tiled=True).astype(
            batch_down.dtype
        ),
    )
    block = whole_up.shape[0] // lax.axis_size("dp")
    offset = lax.axis_index("dp") * block
    grad_up = lax.dynamic_slice_in_dim(whole_up, offset, block, 0)
    grad_down = lax.dynamic_slice_in_dim(whole_down, offset, block, 0)
    return (targets, grad_up, grad_down)


def solution(mesh):
    placed = (
        P("dp", "tm", None),
        P("dp", "tm"),
        P("dp", "tm"),
        P("dp", None, "head"),
        P(),
        P("dp", "head"),
        P("dp", "head"),
    )
    return jax.shard_map(
        local,
        mesh=mesh,
        in_specs=placed,
        out_specs=(P("dp", "tm", "head"), P("dp", "head"), P("dp", "head")),
        check_vma=False,
    )
```

profile of v0, /device:TPU:1, one launch (start us, length us, event | category | flops | bytes accessed | tf_op | source)
XLA Modules:
  0.0 528.7 jit_solution(17435139665778861965)
XLA Ops:
  7.2 2.2 copy.20
  11.0 45.8 %all-gather.7.cloned.1.call-done = bf16[1280,3,160]{2,1,0:T(4,128)(2,1)} async-done(((bf16[320,3,160]{2,1,0:T(4,128)(2,1)}), bf16[1280,3,160]{2,1,0:T(4,128)(2,1)}) %all-gather.7.cloned.1.call-update) | async-done | bytes 1228816 | tf_op jit(solution)/shard_map/all_gather | solution.py:19
  56.7 3.9 copy.21
  62.7 2.3 scatter_custom_fusion
  69.4 22.0 %all-gather.11.cloned.1.call-done = bf16[1280,640]{1,0:T(8,128)(2,1)} async-done(((bf16[320,640]{1,0:T(8,128)(2,1)}), bf16[1280,640]{1,0:T(8,128)(2,1)}) %all-gather.11.cloned.1.call-update) | async-done | bytes 1638416 | tf_op jit(solution)/shard_map/all_gather | solution.py:20
  91.4 1.9 fusion.47
  93.3 32.6 %all-gather.13.cloned.1.call-done = bf16[1280,640]{1,0:T(8,128)(2,1)} async-done(((bf16[320,640]{1,0:T(8,128)(2,1)}), bf16[1280,640]{1,0:T(8,128)(2,1)}) %all-gather.13.cloned.1.call-update) | async-done | bytes 1638416 | tf_op jit(solution)/shard_map/all_gather | solution.py:21
  125.9 3.4 convolution_convert_fusion.2
  129.4 44.4 %all-gather.9.cloned.1.call-done = bf16[4096,2,160]{0,2,1:T(8,128)(2,1)} async-done(((bf16[256,2,160]{0,2,1:T(8,128)(2,1)}), bf16[4096,2,160]{0,2,1:T(8,128)(2,1)}) %all-gather.9.cloned.1.call-update) | async-done | bytes 2621456 | tf_op jit(solution)/shard_map/all_gather | solution.py:35
  173.8 1.9 fusion.52
  177.1 1.5 fusion
  178.6 2.1 fusion.50
  180.9 23.5 %all-reduce = (f32[160]{0:T(256)S(1)}, f32[160]{0:T(256)S(1)}) all-reduce(f32[160]{0:T(256)S(1)} %reduce_sum.65, f32[160]{0:T(256)S(1)} %reduce_sum.63), channel_id=1, replica_groups=mesh['tm'=16,'head'=8,'dp'=4] {'tm'}, use_global_device_ids=true, to_apply=%region_5.0 | all-reduce | flops 320 | bytes 2560 | tf_op jit(solution)/shard_map/psum | solution.py:51
  205.7 20.2 %all_gather.25 = bf16[128,1280]{0,1:T(8,128)(2,1)S(1)} all-gather(bf16[128,160]{0,1:T(8,128)(2,1)S(1)} %select_convert_fusion), channel_id=1, replica_groups=mesh['tm'=16,'head'=8,'dp'=4] {'head'}, dimensions={1}, use_global_device_ids=true | all-gather | bytes 368640 | tf_op jit(solution)/shard_map/all_gather | solution.py:72
  226.1 23.8 %all-reduce.5.cloned.1.call-done = bf16[128,1280]{1,0:T(8,128)(2,1)} async-done(((bf16[128,1280]{1,0:T(8,128)(2,1)}), bf16[128,1280]{1,0:T(8,128)(2,1)}) %all-reduce.5.cloned.1.call-update) | async-done | bytes 327696 | tf_op jit(solution)/shard_map/psum | solution.py:71
  249.8 3.5 convolution_convert_fusion
  254.3 4.3 convolution_convert_fusion.1
  258.6 56.2 %reduce-scatter.5.cloned.1.call-done = bf16[80,640]{1,0:T(8,128)(2,1)} async-done(((bf16[1280,640]{1,0:T(8,128)(2,1)}), bf16[80,640]{1,0:T(8,128)(2,1)}) %reduce-scatter.5.cloned.1.call-update) | async-done | bytes 102416 | tf_op jit(solution)/shard_map/reduce_scatter | solution.py:84
  314.9 62.6 %reduce-scatter.3.cloned.1.call-done = bf16[80,640]{1,0:T(8,128)(2,1)} async-done(((bf16[1280,640]{1,0:T(8,128)(2,1)}), bf16[80,640]{1,0:T(8,128)(2,1)}) %reduce-scatter.3.cloned.1.call-update) | async-done | bytes 102416 | tf_op jit(solution)/shard_map/reduce_scatter | solution.py:81
  377.5 53.7 %all-reduce.7.cloned.1.call-done = (bf16[80,640]{1,0:T(8,128)(2,1)}, bf16[80,640]{1,0:T(8,128)(2,1)}) async-done(((bf16[80,640]{1,0:T(8,128)(2,1)}, bf16[80,640]{1,0:T(8,128)(2,1)}), (bf16[80,640]{1,0:T(8,128)(2,1)}, bf16[80,640]{1,0:T(8,128)(2,1)})) %all-reduce.7.cloned.1.call-update) | async-done | bytes 204816 | tf_op jit(solution)/shard_map/psum | solution.py:89
  432.5 44.8 %all-gather.17.cloned.1.call-done = bf16[1280,640]{1,0:T(8,128)(2,1)} async-done(((bf16[80,640]{1,0:T(8,128)(2,1)}), bf16[1280,640]{1,0:T(8,128)(2,1)}) %all-gather.17.cloned.1.call-update) | async-done | bytes 1638416 | tf_op jit(solution)/shard_map/all_gather | solution.py:96
  477.3 1.9 dynamic-slice_convert_fusion
  479.2 40.6 %all-gather.15.cloned.1.call-done = bf16[1280,640]{1,0:T(8,128)(2,1)} async-done(((bf16[80,640]{1,0:T(8,128)(2,1)}), bf16[1280,640]{1,0:T(8,128)(2,1)}) %all-gather.15.cloned.1.call-update) | async-done | bytes 1638416 | tf_op jit(solution)/shard_map/all_gather | solution.py:93
  519.9 1.9 dynamic-slice_convert_fusion.1
  (68 shorter events, 12.7 us)
Async XLA Ops:
  7.2 53.5 %copy-start = (bf16[1,256,1280]{2,1,0:T(8,128)(2,1)S(1)}, bf16[1,256,1280]{2,1,0:T(8,128)(2,1)}, u32[]{:S(2)}) copy-start(bf16[1,256,1280]{2,1,0:T(8,128)(2,1)} %param.7) | copy-start | bytes 1966084
  7.2 49.5 %all-gather.7.cloned.1.call-start = ((), (), s32[]{:S(2)}) async-start(), calls=%async_computation.2 | async-start | bytes 3276800 | tf_op jit(solution)/shard_map/all_gather | solution.py:19
  9.4 82.0 %all-gather.11.cloned.1.call-start = ((), (), s32[]{:S(2)}) async-start(), calls=%async_computation.4 | async-start | bytes 2048000 | tf_op jit(solution)/shard_map/all_gather | solution.py:20
  10.2 115.7 %all-gather.13.cloned.1.call-start = ((), (), s32[]{:S(2)}) async-start(), calls=%async_computation.5 | async-start | bytes 2048000 | tf_op jit(solution)/shard_map/all_gather | solution.py:21
  10.9 162.9 %all-gather.9.cloned.1.call-start = ((), (), s32[]{:S(2)}) async-start(), calls=%async_computation.3 | async-start | bytes 2785280 | tf_op jit(solution)/shard_map/all_gather | solution.py:35
  60.6 1.4 copy-start.2
  61.2 8.2 %copy-start.1 = (bf16[256,3,160]{0,2,1:T(8,128)(2,1)}, bf16[256,3,160]{0,2,1:T(8,128)(2,1)S(1)}, u32[]{:S(2)}) copy-start(bf16[256,3,160]{0,2,1:T(8,128)(2,1)S(1)} %convert_element_type.75) | copy-start | bytes 737284
  62.0 187.9 %all-reduce.5.cloned.1.call-start = ((), (), s32[]{:S(2)}) async-start(), calls=%async_computation.6 | async-start | bytes 655360 | tf_op jit(solution)/shard_map/psum | solution.py:71
  67.3 24.1 %copy-start.4 = (f32[1280]{0:T(1024)S(1)}, f32[1280]{0:T(1024)}, u32[]{:S(2)}) copy-start(f32[1280]{0:T(1024)} %param.11) | copy-start | bytes 15364
  129.3 46.4 %slice-start = ((bf16[256,3,160]{0,2,1:T(8,128)(2,1)}), bf16[256,1,160]{0,2,1:T(8,128)(2,1)S(1)}, s32[]{:S(2)}) async-start(bf16[256,3,160]{0,2,1:T(8,128)(2,1)} %copy-done.1), calls=%async_computation.12 | async-start | bytes 163840 | tf_op jit(solution)/shard_map/slice | solution.py:29
  129.3 185.5 %reduce-scatter.5.cloned.1.call-start = ((), (), s32[]{:S(2)}) async-start(), calls=%async_computation.9 | async-start | bytes 1740800 | tf_op jit(solution)/shard_map/reduce_scatter | solution.py:84
  253.3 1.0 copy-start.3
  253.3 124.1 %reduce-scatter.3.cloned.1.call-start = ((), (), s32[]{:S(2)}) async-start(), calls=%async_computation.7 | async-start | bytes 1740800 | tf_op jit(solution)/shard_map/reduce_scatter | solution.py:81
  258.6 172.6 %all-reduce.7.cloned.1.call-start = ((), (), s32[]{:S(2)}) async-start(), calls=%async_computation.11 | async-start | bytes 409600 | tf_op jit(solution)/shard_map/psum | solution.py:89
  377.4 99.9 %all-gather.17.cloned.1.call-start = ((), (), s32[]{:S(2)}) async-start(), calls=%async_computation.10 | async-start | bytes 1740800 | tf_op jit(solution)/shard_map/all_gather | solution.py:96
  431.2 88.7 %all-gather.15.cloned.1.call-start = ((), (), s32[]{:S(2)}) async-start(), calls=%async_computation.8 | async-start | bytes 1740800 | tf_op jit(solution)/shard_map/all_gather | solution.py:93
Sparse Core Ops, SparseCore 0:
  10.7 45.9 all-gather.6
  58.8 32.5 all-gather.10
  93.5 32.3 all-gather.12
  127.8 45.9 all-gather.8
  176.5 73.2 all-reduce.4
  253.4 61.3 reduce-scatter.4
  317.7 59.6 reduce-scatter.2
  379.9 51.1 all-reduce.6
  433.3 43.9 all-gather.16
  479.3 40.5 all-gather.14
where the time goes:
time: 529 us
  waiting for transfers between devices  428 us (81%)
  blocking collectives  43.8 us (8%)
  matrix products  17.1 us (3%)
  between operations  15 us (3%)
  local copies, waits for them, and re-layouts  12.2 us (2%)
  other arithmetic  11.8 us (2%)
    reduce_scatter x1, waiting for transfers between devices, local(): lax.psum_scatter(grad_up_term.astype(jnp.bfloat16), 'tm', scatter_dimensi...  62.6 us
    reduce_scatter x1, waiting for transfers between devices, local(): lax.psum_scatter(grad_down_term.astype(jnp.bfloat16), 'tm', scatter_dimen...  56.2 us
    psum x1, waiting for transfers between devices, local(): lax.psum(slice_up.astype(jnp.bfloat16), 'dp').astype(jnp.float32)  53.7 us
    all_gather x1, waiting for transfers between devices, local(): lax.all_gather(teacher_qkv, 'dp', axis=0, tiled=True)  45.8 us
    all_gather x1, waiting for transfers between devices, local(): lax.all_gather(batch_down.astype(jnp.bfloat16), 'tm', axis=0, tiled=True)  44.8 us
    all_gather x1, waiting for transfers between devices, local(): piece = lax.all_gather(paired, 'tm', axis=0, tiled=True)  44.4 us
    all_gather x1, waiting for transfers between devices, local(): lax.all_gather(batch_up.astype(jnp.bfloat16), 'tm', axis=0, tiled=True)  40.6 us
    all_gather x1, waiting for transfers between devices, local(): lax.all_gather(w_down, 'dp', axis=0, tiled=True)  32.6 us
  transfers between devices with their start and end apart: 10, of which 10 were waited for; matrix products, arithmetic and copies ran while one was open for 6% of the time, Pallas kernels for 0%

commit v1 on v0

v1 whole, which is shorter than its diff:
```python
import math

import jax
import jax.numpy as jnp
from jax import lax
from jax.experimental import pallas as pl
from jax.experimental.pallas import tpu as pltpu
from jax.sharding import PartitionSpec as P

BF16 = jnp.bfloat16
F32 = jnp.float32
MESH = pl.DeviceIdType.MESH

D = 1280
HEAD = 80
FRAMES = 256
SLOTS = 128
CHANNELS = 160
HIDDEN = 640
SHARD = 320
NX, NY, NZ = 4, 8, 8
NT = 2 * NY
PIECE = 208
STACK = NY * PIECE
LENGTH = NT * FRAMES
SCALE = HEAD**-0.5


def dot(a, b, dims):
    return lax.dot_general(a, b, (dims, ((), ())), preferred_element_type=F32)


class Names:
    def __init__(self):
        self.index = {}

    def __call__(self, name):
        return self.index.setdefault(name, len(self.index))


def kernel(
    frames_ref,
    masked_ref,
    counts_ref,
    gain_ref,
    wt_ref,
    up_ref,
    down_ref,
    target_ref,
    gup_ref,
    gdown_ref,
    wbuf,
    upbuf,
    downbuf,
    kv,
    normed_ref,
    normed_t,
    act_ref,
    slope_ref,
    dpre_ref,
    psend,
    precv,
    cot,
    stats,
    abuf,
    bbuf,
    g32,
    gs,
    rsb,
    fown,
    foth,
    local_sem,
    send_sem,
    recv_sem,
):
    t = lax.axis_index("tm")
    x = lax.axis_index("dp")
    z = lax.axis_index("head")
    y, c = t // 2, t % 2
    other = 1 - c
    partner = {"tm": y * 2 + other}

    def at_x(step):
        return lax.rem(x + step + NX, NX)

    def at_y(step):
        return lax.rem(y + step + NY, NY)

    def at_z(step):
        return lax.rem(z + step + NZ, NZ)

    barrier = pltpu.get_barrier_semaphore()
    peers = [partner]
    for step in range(1, NY):
        for core in range(2):
            peers.append({"tm": at_y(step) * 2 + core})
    for step in range(1, NX):
        for core in range(2):
            peers.append({"dp": at_x(step), "tm": y * 2 + core})
    for step in range(1, NZ):
        peers.append({"head": at_z(step)})
    for peer in peers:
        pl.semaphore_signal(barrier, inc=1, device_id=peer, device_id_type=MESH)
    pl.semaphore_wait(barrier, len(peers))

    names = Names()
    sent = []

    def describe(src, dst, device, name, out):
        return pltpu.make_async_remote_copy(
            src_ref=src,
            dst_ref=dst,
            send_sem=send_sem.at[out],
            recv_sem=recv_sem.at[name],
            device_id=device,
            device_id_type=MESH,
        )

    def send(src, dst, device, name):
        copy = describe(src, dst, device, names(name), len(sent))
        copy.start()
        sent.append(copy)

    def wait(dst, name):
        describe(dst, dst, partner, names(name), 0).wait_recv()

    def place_w(shard, row, rows):
        return wbuf.at[shard, pl.ds(row, rows), :]

    def place_up(shard, row, rows):
        return upbuf.at[pl.ds(shard * SHARD + row, rows), :]

    def place_down(shard, row, rows):
        return downbuf.at[pl.ds(shard * SHARD + row, rows), :]

    class Gather:
        def __init__(self, name, src, place, half, first, sem):
            self.name, self.src, self.place = name, src, place
            self.half, self.first = half, first
            self.mine, self.theirs = c * half, other * half
            self.own = pltpu.make_async_copy(src, place(x, 0, 2 * half), local_sem.at[sem])

        def start(self):
            self.own.start()
            mine = self.src.at[pl.ds(self.mine, self.half), :]
            there = self.place(x, self.mine, self.half)
            send(mine, there, {"dp": at_x(1)}, self.name + "R0")
            send(mine, there, {"dp": at_x(-1)}, self.name + "L0")

        def relay(self):
            n, first = self.half, self.first
            block = self.place(at_x(-1), self.mine, n)
            wait(block, self.name + "R0")
            part = self.place(at_x(-1), self.mine, first)
            send(part, part, {"dp": at_x(1)}, self.name + "R1")
            send(block, block, partner, self.name + "P0")
            block = self.place(at_x(1), self.mine, n)
            wait(block, self.name + "L0")
            part = self.place(at_x(1), self.mine + first, n - first)
            send(part, part, {"dp": at_x(-1)}, self.name + "L1")
            send(block, block, partner, self.name + "P1")

        def finish(self):
            n, first = self.half, self.first
            far = at_x(2)
            part = self.place(far, self.mine, first)
            wait(part, self.name + "R1")
            send(part, part, partner, self.name + "P2")
            part = self.place(far, self.mine + first, n - first)
            wait(part, self.name + "L1")
            send(part, part, partner, self.name + "P3")
            self.own.wait()
            wait(self.place(at_x(-1), self.theirs, n), self.name + "P0")
            wait(self.place(at_x(1), self.theirs, n), self.name + "P1")
            wait(self.place(far, self.theirs, first), self.name + "P2")
            wait(self.place(far, self.theirs + first, n - first), self.name + "P3")

    teacher = Gather("w", wt_ref, place_w, 240, 128, 0)
    upward = Gather("u", up_ref, place_up, 160, 80, 1)
    downward = Gather("d", down_ref, place_down, 160, 80, 2)

    teacher.start()

    keep = 1 - masked_ref[...]
    keep = keep.astype(F32)
    before = lax.broadcasted_iota(jnp.int32, (FRAMES, FRAMES), 0)
    after = lax.broadcasted_iota(jnp.int32, (FRAMES, FRAMES), 1)
    upper = jnp.where(before <= after, 1.0, 0.0).astype(BF16)
    rank = dot(jnp.broadcast_to(keep, (16, FRAMES)).astype(BF16), upper, ((1,), (0,)))[0:1]
    slot = lax.broadcasted_iota(jnp.int32, (SLOTS, FRAMES), 0).astype(F32)
    pick = jnp.where(rank - 1.0 == slot, jnp.broadcast_to(keep, (SLOTS, FRAMES)), 0.0).astype(BF16)
    chosen = dot(pick, frames_ref[...], ((1,), (0,)))
    centre = jnp.mean(chosen, axis=1, keepdims=True)
    chosen = chosen - centre
    spread = jnp.mean(chosen * chosen, axis=1, keepdims=True)
    normed = chosen * lax.rsqrt(spread + 1e-5) * gain_ref[...]
    normed_ref[...] = normed.astype(BF16)
    normed_t[...] = normed.T.astype(BF16)

    teacher.relay()
    upward.start()
    teacher.finish()

    qkv = jnp.zeros((3 * CHANNELS, FRAMES), F32)
    for shard in range(NX):
        qkv = qkv + dot(
            wbuf[shard], frames_ref[:, shard * SHARD : (shard + 1) * SHARD], ((1,), (1,))
        )
    qkv = qkv.astype(BF16)
    kv[y, c] = qkv[CHANNELS:]
    query = [qkv[h * HEAD : (h + 1) * HEAD] for h in range(2)]

    def block(source, core, part):
        return kv.at[source, core, pl.ds(part * CHANNELS, CHANNELS), :]

    right, left = {"tm": at_y(1) * 2 + c}, {"tm": at_y(-1) * 2 + c}
    for part, tag in ((0, "k"), (1, "v")):
        mine = block(y, c, part)
        send(mine, mine, right, tag + "R0")
        send(mine, mine, left, tag + "L0")
        send(mine, mine, partner, tag + "P0")

    best = [jnp.full((1, FRAMES), -jnp.inf, F32) for _ in range(2)]
    accum = [jnp.zeros((HEAD + 16, FRAMES), F32) for _ in range(2)]

    def attend(blocks):
        for h in range(2):
            keys = jnp.concatenate(
                [kv[s, core, h * HEAD : (h + 1) * HEAD, :] for s, core in blocks], axis=1
            )
            low = CHANNELS + h * HEAD
            values = jnp.concatenate(
                [kv[s, core, low : low + HEAD, :] for s, core in blocks], axis=1
            )
            values = jnp.concatenate([values, jnp.ones((16, values.shape[1]), BF16)], axis=0)
            scores = dot(keys, query[h], ((0,), (0,)))
            top = jnp.maximum(best[h], jnp.max(scores, axis=0, keepdims=True))
            fade = jnp.exp((best[h] - top) * SCALE)
            weights = jnp.exp((scores - top) * SCALE).astype(BF16)
            accum[h] = accum[h] * fade + dot(values, weights, ((1,), (0,)))
            best[h] = top

    def forward(step):
        behind, ahead = at_y(-step), at_y(step)
        for part, tag in ((0, "k"), (1, "v")):
            if step < 4 or part == 0:
                here = block(behind, c, part)
                wait(here, f"{tag}R{step - 1}")
                if step < 3 or (step == 3 and part == 0):
                    send(here, here, right, f"{tag}R{step}")
                send(here, here, partner, f"{tag}PR{step}")
            if step < 4 or part == 1:
                here = block(ahead, c, part)
                wait(here, f"{tag}L{step - 1}")
                if step < 3 or (step == 3 and part == 1):
                    send(here, here, left, f"{tag}L{step}")
                send(here, here, partner, f"{tag}PL{step}")

    def shared(step):
        for part, tag in ((0, "k"), (1, "v")):
            if step == 0:
                wait(block(y, other, part), tag + "P0")
                continue
            if step < 4 or part == 0:
                wait(block(at_y(-step), other, part), f"{tag}PR{step}")
            if step < 4 or part == 1:
                wait(block(at_y(step), other, part), f"{tag}PL{step}")

    me = x * 2 + c

    def operand(tag, role, source, target):
        for step in range(1, NX):
            out = len(sent)
            sem = names(f"{tag}{step}0")
            names(f"{tag}{step}1")
            copy = describe(
                source(at_x(step)), target.at[me], {"dp": at_x(step), "tm": y * 2 + role}, sem + c, out
            )
            copy.start()
            sent.append(copy)
        sem = names(f"{tag}00")
        names(f"{tag}01")
        out = len(sent)
        copy = describe(source(x), target.at[me], partner, sem + c, out)

        @pl.when(c == role)
        def _():
            target[me] = source(x)[...]

        @pl.when(c != role)
        def _():
            copy.start()

        sent.append((role, copy))

    def operands_here(tag, target):
        sem = names(f"{tag}00")
        describe(
            target.at[x * 2 + other], target.at[x * 2 + other], partner, sem + other, 0
        ).wait_recv()
        for step in range(1, NX):
            for core in range(2):
                here = target.at[at_x(-step) * 2 + core]
                describe(here, here, partner, names(f"{tag}{step}{core}"), 0).wait_recv()

    attend([(y, c)])
    shared(0)
    attend([(y, other)])
    forward(1)
    upward.relay()
    downward.start()
    attend([(at_y(-1), c), (at_y(1), c)])
    shared(1)
    attend([(at_y(-1), other), (at_y(1), other)])
    forward(2)
    upward.finish()
    attend([(at_y(-2), c), (at_y(2), c)])
    shared(2)

    pre = dot(normed_ref[...], upbuf[...], ((1,), (0,)))
    cumulative = 0.5 * (1.0 + lax.erf(pre * math.sqrt(0.5)))
    act_ref[...] = (pre * cumulative).astype(BF16)
    slope_ref[...] = cumulative + pre * (jnp.exp(-0.5 * pre * pre) * (1.0 / math.sqrt(2 * math.pi)))

    forward(3)
    downward.relay()
    operand("b", 0, lambda to: act_ref, bbuf)
    operand("a", 1, lambda to: normed_t.at[pl.ds(to * SHARD, SHARD), :], abuf)
    attend([(at_y(-2), other), (at_y(2), other)])
    attend([(at_y(-3), c), (at_y(3), c)])
    forward(4)
    downward.finish()

    psend[...] = dot(downbuf[...], act_ref[...], ((1,), (1,))).astype(BF16)
    for step in range(1, NZ):
        to = at_z(step)
        send(
            psend.at[pl.ds(to * CHANNELS, CHANNELS), :],
            precv.at[z],
            {"head": to},
            f"p{step}",
        )
    shared(3)
    attend([(at_y(-3), other), (at_y(3), other), (at_y(4), c)])
    shared(4)
    attend([(at_y(4), other)])

    context = [accum[h][:HEAD] / accum[h][HEAD : HEAD + 1] for h in range(2)]
    lane = lax.broadcasted_iota(jnp.int32, (HEAD, 128), 1)
    columns = jnp.zeros((HEAD, 128), F32)
    for h in range(2):
        first = jnp.sum(context[h], axis=1, keepdims=True)
        second = jnp.sum(context[h] * context[h], axis=1, keepdims=True)
        columns = jnp.where(lane == h, first, jnp.where(lane == 2 + h, second, columns))
    columns = jnp.concatenate([columns, jnp.zeros((128 - HEAD, 128), F32)], axis=0)
    stats[0] = columns.T[0:8]
    for step in range(1, NT):
        send(stats.at[0], stats.at[step], {"tm": lax.rem(t + step, NT)}, f"s{step}")
    total = stats[0]
    for step in range(1, NT):
        wait(stats.at[step], f"s{step}")
        total = total + stats[step]
    columns = jnp.concatenate([total, jnp.zeros((120, 128), F32)], axis=0).T
    parts = []
    for h in range(2):
        mean = columns[:HEAD, h : h + 1] * (1.0 / LENGTH)
        var = columns[:HEAD, 2 + h : 3 + h] * (1.0 / LENGTH) - mean * mean
        parts.append((context[h] - mean) * lax.rsqrt(var + 1e-5))
    target = jnp.concatenate(parts, axis=0).astype(BF16)
    target_ref[...] = target

    aim = dot(target, pick, ((1,), (1,)))
    pred = psend[pl.ds(z * CHANNELS, CHANNELS), :].astype(F32)
    for step in range(1, NZ):
        wait(precv.at[at_z(-step)], f"p{step}")
        pred = pred + precv[at_z(-step)].astype(F32)
    number = lax.broadcasted_iota(jnp.int32, (CHANNELS, SLOTS), 1)
    valid = number < jnp.broadcast_to(counts_ref[...], (CHANNELS, SLOTS))
    gap = jnp.where(valid, pred - aim, 0.0) * (2.0 / math.sqrt(D))
    here = cot.at[pl.ds(z * CHANNELS, CHANNELS), :]
    here[...] = gap.astype(BF16)
    for step in range(1, NZ):
        send(here, here, {"head": at_z(step)}, f"c{step}")
    for step in range(1, NZ):
        wait(cot.at[pl.ds(at_z(-step) * CHANNELS, CHANNELS), :], f"c{step}")

    operand("a", 0, lambda to: cot.at[pl.ds(to * SHARD, SHARD), :], abuf)
    back = dot(cot[...], downbuf[...], ((0,), (0,)))
    dpre_ref[...] = (back * slope_ref[...]).astype(BF16)
    operand("b", 1, lambda to: dpre_ref, bbuf)

    operands_here("a", abuf)
    operands_here("b", bbuf)
    grad = jnp.zeros((SHARD, HIDDEN), F32)
    for pair in range(NX):
        rows = jnp.concatenate([abuf[2 * pair], abuf[2 * pair + 1]], axis=1)
        columns = jnp.concatenate([bbuf[2 * pair], bbuf[2 * pair + 1]], axis=0)
        grad = grad + dot(rows, columns, ((1,), (0,)))
    for band in range(HIDDEN // 128):
        stripe = grad[:, band * 128 : (band + 1) * 128]
        g32[band * SHARD : (band + 1) * SHARD, :] = stripe
        gs[band * SHARD : (band + 1) * SHARD, :] = stripe.astype(BF16)
    rest = STACK - SHARD * HIDDEN // 128
    g32[STACK - rest :, :] = jnp.zeros((rest, 128), F32)
    gs[STACK - rest :, :] = jnp.zeros((rest, 128), BF16)

    for step in range(1, NY):
        to = at_y(step)
        send(gs.at[pl.ds(to * PIECE, PIECE), :], rsb.at[step - 1], {"tm": to * 2 + c}, f"r{step}")
    total = g32[pl.ds(y * PIECE, PIECE), :]
    for step in range(1, NY):
        wait(rsb.at[step - 1], f"r{step}")
        total = total + rsb[step - 1].astype(F32)
    here = fown.at[pl.ds(y * PIECE, PIECE), :]
    here[...] = total.astype(BF16)
    for step in range(1, NY):
        send(here, here, {"tm": at_y(step) * 2 + c}, f"g{step}")
    send(here, foth.at[pl.ds(y * PIECE, PIECE), :], partner, "h0")
    for step in range(1, NY):
        rows = pl.ds(at_y(-step) * PIECE, PIECE)
        wait(fown.at[rows, :], f"g{step}")
        send(fown.at[rows, :], foth.at[rows, :], partner, f"h{step}")
    for step in range(NY):
        wait(foth.at[pl.ds(at_y(-step) * PIECE, PIECE), :], f"h{step}")

    def unstack(source, out):
        for band in range(HIDDEN // 128):
            out[:, band * 128 : (band + 1) * 128] = source[band * SHARD : (band + 1) * SHARD, :]

    @pl.when(c == 0)
    def _():
        unstack(fown, gdown_ref)
        unstack(foth, gup_ref)

    @pl.when(c != 0)
    def _():
        unstack(fown, gup_ref)
        unstack(foth, gdown_ref)

    for copy in sent:
        if isinstance(copy, tuple):
            role, copy = copy

            @pl.when(c != role)
            def _():
                copy.wait_send()
        else:
            copy.wait_send()


def local(frames, masked, kept_counts, teacher_qkv, student_gain, w_up, w_down):
    wt = teacher_qkv.transpose(1, 2, 0).reshape(3 * CHANNELS, SHARD)
    vmem = pl.BlockSpec(memory_space=pltpu.VMEM)
    hbm = pl.BlockSpec(memory_space=pl.ANY)
    target, gup, gdown = pl.pallas_call(
        kernel,
        out_shape=(
            jax.ShapeDtypeStruct((CHANNELS, FRAMES), BF16),
            jax.ShapeDtypeStruct((SHARD, HIDDEN), BF16),
            jax.ShapeDtypeStruct((SHARD, HIDDEN), BF16),
        ),
        in_specs=[vmem, vmem, vmem, vmem, hbm, hbm, hbm],
        out_specs=(vmem, vmem, vmem),
        scratch_shapes=[
            pltpu.VMEM((NX, 3 * CHANNELS, SHARD), BF16),
            pltpu.VMEM((D, HIDDEN), BF16),
            pltpu.VMEM((D, HIDDEN), BF16),
            pltpu.VMEM((NY, 2, 2 * CHANNELS, FRAMES), BF16),
            pltpu.VMEM((SLOTS, D), BF16),
            pltpu.VMEM((D, SLOTS), BF16),
            pltpu.VMEM((SLOTS, HIDDEN), BF16),
            pltpu.VMEM((SLOTS, HIDDEN), F32),
            pltpu.VMEM((SLOTS, HIDDEN), BF16),
            pltpu.VMEM((D, SLOTS), BF16),
            pltpu.VMEM((NZ, CHANNELS, SLOTS), BF16),
            pltpu.VMEM((D, SLOTS), BF16),
            pltpu.VMEM((NT, 8, 128), F32),
            pltpu.VMEM((2 * NX, SHARD, SLOTS), BF16),
            pltpu.VMEM((2 * NX, SLOTS, HIDDEN), BF16),
            pltpu.VMEM((STACK, 128), F32),
            pltpu.VMEM((STACK, 128), BF16),
            pltpu.VMEM((NY - 1, PIECE, 128), BF16),
            pltpu.VMEM((STACK, 128), BF16),
            pltpu.VMEM((STACK, 128), BF16),
            pltpu.SemaphoreType.DMA((3,)),
            pltpu.SemaphoreType.DMA((192,)),
            pltpu.SemaphoreType.DMA((160,)),
        ],
        compiler_params=pltpu.CompilerParams(
            collective_id=0, has_side_effects=True, vmem_limit_bytes=48 * 1024 * 1024
        ),
    )(
        frames[0],
        masked,
        kept_counts,
        student_gain[None],
        wt,
        w_up,
        w_down,
    )
    return target.T[None], gup.astype(F32), gdown.astype(F32)


def solution(mesh):
    placed = (
        P("dp", "tm", None),
        P("dp", "tm"),
        P("dp", "tm"),
        P("dp", None, "head"),
        P(),
        P("dp", "head"),
        P("dp", "head"),
    )
    return jax.shard_map(
        local,
        mesh=mesh,
        in_specs=placed,
        out_specs=(P("dp", "tm", "head"), P("dp", "head"), P("dp", "head")),
        check_vma=False,
    )
```

time: 529 us -> 118 us (0.22)
  waiting for transfers between devices: 428 us -> 0 us
  Pallas kernels: 0 us -> 109 us
  blocking collectives: 43.8 us -> 0 us
  matrix products: 17.1 us -> 0 us
  between operations: 15 us -> 1.3 us
  other arithmetic: 11.8 us -> 1.89 us
  local copies, waits for them, and re-layouts: 12.2 us -> 5.42 us
    all_gather x6 -> x0, waiting for transfers between devices: 230 us -> none  [the longest x1 45.8 us: local(): lax.all_gather(teacher_qkv, 'dp', axis=0, tiled=True)]
    reduce_scatter x2 -> x0, waiting for transfers between devices: 119 us -> none  [the longest x1 62.6 us: local(): lax.psum_scatter(grad_up_term.astype(jnp.bfloat16), 'tm', scatter_dimensi...]
    pallas_call x0 -> x1, Pallas kernels: none -> 109 us  [local(): pl.pallas_call(kernel, out_shape=(jax.ShapeDtypeStruct((CHANNELS, FRAMES)...]
    psum x2 -> x0, waiting for transfers between devices: 77.4 us -> none  [the longest x1 53.7 us: local(): lax.psum(slice_up.astype(jnp.bfloat16), 'dp').astype(jnp.float32)]
    psum x1 -> x0, blocking collectives: 23.5 us -> none  [local(): lax.psum((jnp.sum(context, axis=0), jnp.sum(context * context, axis=0)),...]
    all_gather x1 -> x0, blocking collectives: 20.2 us -> none  [local(): lax.all_gather(aim.astype(jnp.bfloat16), 'head', axis=1, tiled=True)]
    dot_general x6 -> x0, matrix products: 16.5 us -> none  [the longest x1 4.31 us: local(): jnp.einsum('cd,cf->df', normed, d_pre, preferred_element_type=jnp.float32)]
  transfers between devices with their start and end apart: 10 -> 0, of which waited for: 10 -> 0; matrix products, arithmetic and copies ran while one was open for 6% -> 0% of each run, Pallas kernels for 0% -> 0%
where the time goes in v1:
time: 118 us; the launch traced here: 117 us
  Pallas kernels  109 us (92%)
  local copies, waits for them, and re-layouts  5.42 us (5%)
  other arithmetic  1.89 us (2%)
  between operations  1.3 us (1%)
    pallas_call x1, Pallas kernels, local(): pl.pallas_call(kernel, out_shape=(jax.ShapeDtypeStruct((CHANNELS, FRAMES)...  109 us
    unnamed x11, local copies, waits for them, and re-layouts  4.71 us

profile of v1, /device:TPU:1, one launch (start us, length us, event | category | flops | bytes accessed | tf_op | source)
XLA Modules:
  0.0 117.5 jit_solution(2331613883070190361)
XLA Ops:
  1.3 0.0 copy-start.4
  1.3 0.7 broadcast_in_dim.6.gain_ref
  2.0 0.0 copy-done.4
  2.0 0.0 copy-start
  2.0 1.1 copy-done
  3.1 0.0 copy-start.1
  3.1 1.0 copy-done.1
  4.1 0.0 copy-start.2
  4.1 1.0 copy-done.2
  5.1 0.0 copy-start.3
  5.1 1.0 copy-done.3
  6.1 108.9 %shard_map.94 = (bf16[160,256]{1,0:T(8,128)(2,1)S(1)}, bf16[320,640]{1,0:T(8,128)(2,1)S(1)}, bf16[320,640]{1,0:T(8,128)(2,1)S(1)}) custom-call(bf16[256,1280]{1,0:T(8,128)(2,1)S(1)} %bitcast.7, s32[1,256]{1,0:T(1,128)S(1)} %copy-done.4, s32[1,1]{1,0:T(1,128)S(6)} %copy.11.counts_ref, f32[1,1280]{1,0:T(1,128)S(1)} %broadcast_in_dim.6.gain_ref, ...), custom_call_target="tpu_custom_call" | custom-call | tf_op jit(solution)/shard_map/pallas_call | solution.py:455
  115.0 0.9 convert_element_type.6
  115.9 0.9 convert_element_type.7
  116.8 0.6 copy.12
Async XLA Ops:
  1.3 0.7 copy-start.4
  2.0 1.1 copy-start
  3.1 1.0 copy-start.1
  4.1 1.0 copy-start.2
  5.1 1.0 copy-start.3

commit v2 on v1

--- a/solution.py
+++ b/solution.py
@@ -22,6 +22,8 @@
 NT = 2 * NY
 PIECE = 208
 STACK = NY * PIECE
+CHUNKS = ((0, 2, 80), (2, 2, 80), (4, 1, 48))
+NEAR = (1, 3, 2)
 LENGTH = NT * FRAMES
 SCALE = HEAD**-0.5
 
@@ -39,7 +41,7 @@
 
 
 def kernel(
-    frames_ref,
+    frames_hbm,
     masked_ref,
     counts_ref,
     gain_ref,
@@ -49,6 +51,7 @@
     target_ref,
     gup_ref,
     gdown_ref,
+    frames_ref,
     wbuf,
     upbuf,
     downbuf,
@@ -89,6 +92,9 @@
     def at_z(step):
         return lax.rem(z + step + NZ, NZ)
 
+    fetch = pltpu.make_async_copy(frames_hbm, frames_ref, local_sem.at[4])
+    fetch.start()
+
     barrier = pltpu.get_barrier_semaphore()
     peers = [partner]
     for step in range(1, NY):
@@ -133,7 +139,33 @@
     def place_down(shard, row, rows):
         return downbuf.at[pl.ds(shard * SHARD + row, rows), :]
 
-    class Gather:
+    class Direct:
+        def __init__(self, name, src, place, base, half, sem):
+            self.name, self.src, self.place, self.half = name, src, place, half
+            self.mine, self.theirs = base + c * half, base + other * half
+            self.own = pltpu.make_async_copy(
+                src.at[pl.ds(base, 2 * half), :], place(x, base, 2 * half), local_sem.at[sem]
+            )
+
+        def start(self):
+            mine = self.src.at[pl.ds(self.mine, self.half), :]
+            there = self.place(x, self.mine, self.half)
+            for step in NEAR:
+                send(mine, there, {"dp": at_x(step)}, f"{self.name}{step}")
+            self.own.start()
+
+        def share(self):
+            for step in NEAR:
+                block = self.place(at_x(-step), self.mine, self.half)
+                wait(block, f"{self.name}{step}")
+                send(block, block, partner, f"{self.name}P{step}")
+
+        def finish(self):
+            self.own.wait()
+            for step in NEAR:
+                wait(self.place(at_x(-step), self.theirs, self.half), f"{self.name}P{step}")
+
+    class Relay:
         def __init__(self, name, src, place, half, first, sem):
             self.name, self.src, self.place = name, src, place
             self.half, self.first = half, first
@@ -141,11 +173,11 @@
             self.own = pltpu.make_async_copy(src, place(x, 0, 2 * half), local_sem.at[sem])
 
         def start(self):
-            self.own.start()
             mine = self.src.at[pl.ds(self.mine, self.half), :]
             there = self.place(x, self.mine, self.half)
             send(mine, there, {"dp": at_x(1)}, self.name + "R0")
             send(mine, there, {"dp": at_x(-1)}, self.name + "L0")
+            self.own.start()
 
         def relay(self):
             n, first = self.half, self.first
@@ -160,7 +192,7 @@
             send(part, part, {"dp": at_x(-1)}, self.name + "L1")
             send(block, block, partner, self.name + "P1")
 
-        def finish(self):
+        def share(self):
             n, first = self.half, self.first
             far = at_x(2)
             part = self.place(far, self.mine, first)
@@ -169,17 +201,24 @@
             part = self.place(far, self.mine + first, n - first)
             wait(part, self.name + "L1")
             send(part, part, partner, self.name + "P3")
+
+        def near(self):
+            n = self.half
             self.own.wait()
             wait(self.place(at_x(-1), self.theirs, n), self.name + "P0")
             wait(self.place(at_x(1), self.theirs, n), self.name + "P1")
-            wait(self.place(far, self.theirs, first), self.name + "P2")
-            wait(self.place(far, self.theirs + first, n - first), self.name + "P3")
-
-    teacher = Gather("w", wt_ref, place_w, 240, 128, 0)
-    upward = Gather("u", up_ref, place_up, 160, 80, 1)
-    downward = Gather("d", down_ref, place_down, 160, 80, 2)
-
-    teacher.start()
+
+        def far(self):
+            n, first = self.half, self.first
+            wait(self.place(at_x(2), self.theirs, first), self.name + "P2")
+            wait(self.place(at_x(2), self.theirs + first, n - first), self.name + "P3")
+
+    teacher_kv = Direct("w", wt_ref, place_w, CHANNELS, CHANNELS, 0)
+    teacher_q = Direct("q", wt_ref, place_w, 0, HEAD, 3)
+    upward = Relay("u", up_ref, place_up, 160, 80, 1)
+    downward = Relay("d", down_ref, place_down, 160, 80, 2)
+
+    teacher_kv.start()
 
     keep = 1 - masked_ref[...]
     keep = keep.astype(F32)
@@ -189,36 +228,42 @@
     rank = dot(jnp.broadcast_to(keep, (16, FRAMES)).astype(BF16), upper, ((1,), (0,)))[0:1]
     slot = lax.broadcasted_iota(jnp.int32, (SLOTS, FRAMES), 0).astype(F32)
     pick = jnp.where(rank - 1.0 == slot, jnp.broadcast_to(keep, (SLOTS, FRAMES)), 0.0).astype(BF16)
+    fetch.wait()
     chosen = dot(pick, frames_ref[...], ((1,), (0,)))
     centre = jnp.mean(chosen, axis=1, keepdims=True)
     chosen = chosen - centre
     spread = jnp.mean(chosen * chosen, axis=1, keepdims=True)
-    normed = chosen * lax.rsqrt(spread + 1e-5) * gain_ref[...]
+    normed = chosen * lax.rsqrt(spread + 1e-5) * gain_ref[...].reshape(1, D)
     normed_ref[...] = normed.astype(BF16)
     normed_t[...] = normed.T.astype(BF16)
 
-    teacher.relay()
-    upward.start()
-    teacher.finish()
-
-    qkv = jnp.zeros((3 * CHANNELS, FRAMES), F32)
-    for shard in range(NX):
-        qkv = qkv + dot(
-            wbuf[shard], frames_ref[:, shard * SHARD : (shard + 1) * SHARD], ((1,), (1,))
-        )
-    qkv = qkv.astype(BF16)
-    kv[y, c] = qkv[CHANNELS:]
-    query = [qkv[h * HEAD : (h + 1) * HEAD] for h in range(2)]
+    def project(low, high):
+        out = jnp.zeros((high - low, FRAMES), F32)
+        for shard in range(NX):
+            out = out + dot(
+                wbuf[shard, low:high, :], frames_ref[:, shard * SHARD : (shard + 1) * SHARD], ((1,), (1,))
+            )
+        return out.astype(BF16)
 
     def block(source, core, part):
         return kv.at[source, core, pl.ds(part * CHANNELS, CHANNELS), :]
 
+    teacher_kv.share()
+    teacher_q.start()
+    teacher_kv.finish()
+    kv[y, c] = project(CHANNELS, 3 * CHANNELS)
     right, left = {"tm": at_y(1) * 2 + c}, {"tm": at_y(-1) * 2 + c}
     for part, tag in ((0, "k"), (1, "v")):
         mine = block(y, c, part)
         send(mine, mine, right, tag + "R0")
         send(mine, mine, left, tag + "L0")
         send(mine, mine, partner, tag + "P0")
+    upward.start()
+    teacher_q.share()
+    teacher_q.finish()
+    downward.start()
+    query = project(0, CHANNELS)
+    query = [query[h * HEAD : (h + 1) * HEAD] for h in range(2)]
 
     best = [jnp.full((1, FRAMES), -jnp.inf, F32) for _ in range(2)]
     accum = [jnp.zeros((HEAD + 16, FRAMES), F32) for _ in range(2)]
@@ -268,80 +313,63 @@
 
     me = x * 2 + c
 
-    def operand(tag, role, source, target):
-        for step in range(1, NX):
-            out = len(sent)
+    def operand(tag, role, source, place):
+        for step in NEAR:
             sem = names(f"{tag}{step}0")
             names(f"{tag}{step}1")
             copy = describe(
-                source(at_x(step)), target.at[me], {"dp": at_x(step), "tm": y * 2 + role}, sem + c, out
+                source(at_x(step)), place(me), {"dp": at_x(step), "tm": y * 2 + role}, sem + c, len(sent)
             )
             copy.start()
             sent.append(copy)
         sem = names(f"{tag}00")
         names(f"{tag}01")
-        out = len(sent)
-        copy = describe(source(x), target.at[me], partner, sem + c, out)
+        copy = describe(source(x), place(me), partner, sem + c, len(sent))
 
         @pl.when(c == role)
         def _():
-            target[me] = source(x)[...]
+            place(me)[...] = source(x)[...]
 
         @pl.when(c != role)
         def _():
             copy.start()
 
-        sent.append((role, copy))
-
-    def operands_here(tag, target):
-        sem = names(f"{tag}00")
-        describe(
-            target.at[x * 2 + other], target.at[x * 2 + other], partner, sem + other, 0
-        ).wait_recv()
-        for step in range(1, NX):
+        sent.append((c != role, copy))
+
+    def operand_here(tag, place):
+        here = place(x * 2 + other)
+        describe(here, here, partner, names(f"{tag}00") + other, 0).wait_recv()
+        for step in NEAR:
             for core in range(2):
-                here = target.at[at_x(-step) * 2 + core]
+                here = place(at_x(-step) * 2 + core)
                 describe(here, here, partner, names(f"{tag}{step}{core}"), 0).wait_recv()
+
+    def whole_a(source):
+        return abuf.at[source]
+
+    def whole_b(source):
+        return bbuf.at[source]
 
     attend([(y, c)])
     shared(0)
     attend([(y, other)])
     forward(1)
-    upward.relay()
-    downward.start()
     attend([(at_y(-1), c), (at_y(1), c)])
     shared(1)
     attend([(at_y(-1), other), (at_y(1), other)])
     forward(2)
-    upward.finish()
+    upward.relay()
     attend([(at_y(-2), c), (at_y(2), c)])
     shared(2)
-
-    pre = dot(normed_ref[...], upbuf[...], ((1,), (0,)))
-    cumulative = 0.5 * (1.0 + lax.erf(pre * math.sqrt(0.5)))
-    act_ref[...] = (pre * cumulative).astype(BF16)
-    slope_ref[...] = cumulative + pre * (jnp.exp(-0.5 * pre * pre) * (1.0 / math.sqrt(2 * math.pi)))
-
+    attend([(at_y(-2), other), (at_y(2), other)])
     forward(3)
     downward.relay()
-    operand("b", 0, lambda to: act_ref, bbuf)
-    operand("a", 1, lambda to: normed_t.at[pl.ds(to * SHARD, SHARD), :], abuf)
-    attend([(at_y(-2), other), (at_y(2), other)])
     attend([(at_y(-3), c), (at_y(3), c)])
+    upward.share()
+    shared(3)
+    attend([(at_y(-3), other), (at_y(3), other)])
     forward(4)
-    downward.finish()
-
-    psend[...] = dot(downbuf[...], act_ref[...], ((1,), (1,))).astype(BF16)
-    for step in range(1, NZ):
-        to = at_z(step)
-        send(
-            psend.at[pl.ds(to * CHANNELS, CHANNELS), :],
-            precv.at[z],
-            {"head": to},
-            f"p{step}",
-        )
-    shared(3)
-    attend([(at_y(-3), other), (at_y(3), other), (at_y(4), c)])
+    attend([(at_y(4), c)])
     shared(4)
     attend([(at_y(4), other)])
 
@@ -356,6 +384,44 @@
     stats[0] = columns.T[0:8]
     for step in range(1, NT):
         send(stats.at[0], stats.at[step], {"tm": lax.rem(t + step, NT)}, f"s{step}")
+
+    downward.share()
+    upward.near()
+    upward.far()
+    pre = dot(normed_ref[...], upbuf[...], ((1,), (0,)))
+    cumulative = 0.5 * (1.0 + lax.erf(pre * math.sqrt(0.5)))
+    act_ref[...] = (pre * cumulative).astype(BF16)
+    slope_ref[...] = cumulative + pre * (jnp.exp(-0.5 * pre * pre) * (1.0 / math.sqrt(2 * math.pi)))
+
+    def predict(shard, step):
+        rows = pl.ds(shard * SHARD, SHARD)
+        psend[rows, :] = dot(downbuf[rows, :], act_ref[...], ((1,), (1,))).astype(BF16)
+        for half in range(2):
+            to = shard * 2 + half
+            copy = describe(
+                psend.at[pl.ds(to * CHANNELS, CHANNELS), :],
+                precv.at[z],
+                {"head": to},
+                names("p0") + lax.rem(to - z + NZ, NZ),
+                len(sent),
+            )
+
+            @pl.when(to != z)
+            def _():
+                copy.start()
+
+            sent.append((to != z, copy))
+
+    for step in range(NZ):
+        names(f"p{step}")
+    downward.near()
+    for step in (0, 1, 3):
+        predict(at_x(step), step)
+    downward.far()
+    predict(at_x(2), 2)
+    operand("act", 0, lambda to: act_ref, whole_b)
+    operand("nrm", 1, lambda to: normed_t.at[pl.ds(to * SHARD, SHARD), :], whole_a)
+
     total = stats[0]
     for step in range(1, NT):
         wait(stats.at[step], f"s{step}")
@@ -379,49 +445,126 @@
     gap = jnp.where(valid, pred - aim, 0.0) * (2.0 / math.sqrt(D))
     here = cot.at[pl.ds(z * CHANNELS, CHANNELS), :]
     here[...] = gap.astype(BF16)
-    for step in range(1, NZ):
+    for step in (1, 7, 2, 6, 3, 5, 4):
         send(here, here, {"head": at_z(step)}, f"c{step}")
-    for step in range(1, NZ):
-        wait(cot.at[pl.ds(at_z(-step) * CHANNELS, CHANNELS), :], f"c{step}")
-
-    operand("a", 0, lambda to: cot.at[pl.ds(to * SHARD, SHARD), :], abuf)
-    back = dot(cot[...], downbuf[...], ((0,), (0,)))
+
+    for step in range(4 * NX):
+        names(f"e{step}")
+
+    def half_a(source, half):
+        return abuf.at[source, pl.ds(half * CHANNELS, CHANNELS), :]
+
+    def pass_on(owner):
+        to, half = owner // 2, lax.rem(owner, 2)
+        source = cot.at[pl.ds(owner * CHANNELS, CHANNELS), :]
+        sem = names("e0") + lax.rem(to - x + NX, NX) * 4 + c * 2 + half
+        copy = describe(source, half_a(me, half), {"dp": to, "tm": y * 2}, sem, len(sent))
+        mine = jnp.logical_and(to == x, c == 0)
+        away = jnp.logical_not(mine)
+
+        @pl.when(mine)
+        def _():
+            half_a(me, half)[...] = source[...]
+
+        @pl.when(away)
+        def _():
+            copy.start()
+
+        sent.append((away, copy))
+
+    def back_from(owner):
+        rows = pl.ds(owner * CHANNELS, CHANNELS)
+        return dot(cot[rows, :], downbuf[rows, :], ((0,), (0,)))
+
+    pass_on(z)
+    back = back_from(z)
+    for step in (1, 7, 2, 6, 3, 5, 4):
+        owner = at_z(-step)
+        wait(cot.at[pl.ds(owner * CHANNELS, CHANNELS), :], f"c{step}")
+        pass_on(owner)
+        back = back + back_from(owner)
     dpre_ref[...] = (back * slope_ref[...]).astype(BF16)
-    operand("b", 1, lambda to: dpre_ref, bbuf)
-
-    operands_here("a", abuf)
-    operands_here("b", bbuf)
-    grad = jnp.zeros((SHARD, HIDDEN), F32)
-    for pair in range(NX):
-        rows = jnp.concatenate([abuf[2 * pair], abuf[2 * pair + 1]], axis=1)
-        columns = jnp.concatenate([bbuf[2 * pair], bbuf[2 * pair + 1]], axis=0)
-        grad = grad + dot(rows, columns, ((1,), (0,)))
-    for band in range(HIDDEN // 128):
-        stripe = grad[:, band * 128 : (band + 1) * 128]
-        g32[band * SHARD : (band + 1) * SHARD, :] = stripe
-        gs[band * SHARD : (band + 1) * SHARD, :] = stripe.astype(BF16)
+    for number, (band, bands, _) in enumerate(CHUNKS):
+        columns = pl.ds(band * 128, bands * 128)
+        operand(
+            f"m{number}",
+            1,
+            lambda to: dpre_ref.at[:, columns],
+            lambda source: bbuf.at[source, :, columns],
+        )
+
+    @pl.when(c == 0)
+    def _():
+        operand_here("act", whole_b)
+        for step in (0, *NEAR):
+            for core in range(2):
+                for half in range(2):
+                    here = half_a(at_x(-step) * 2 + core, half)
+                    copy = describe(
+                        here, here, partner, names("e0") + step * 4 + core * 2 + half, 0
+                    )
+                    if (step, core) != (0, 0):
+                        copy.wait_recv()
+
+    @pl.when(c != 0)
+    def _():
+        operand_here("nrm", whole_a)
+
+    def eighth(number, which):
+        band, _, rows = CHUNKS[number]
+        return pl.ds(band * SHARD + which * rows, rows)
+
+    def landing(number, step):
+        band, _, rows = CHUNKS[number]
+        return rsb.at[step - 1, pl.ds(band * SHARD // NY, rows), :]
+
     rest = STACK - SHARD * HIDDEN // 128
     g32[STACK - rest :, :] = jnp.zeros((rest, 128), F32)
     gs[STACK - rest :, :] = jnp.zeros((rest, 128), BF16)
-
-    for step in range(1, NY):
-        to = at_y(step)
-        send(gs.at[pl.ds(to * PIECE, PIECE), :], rsb.at[step - 1], {"tm": to * 2 + c}, f"r{step}")
-    total = g32[pl.ds(y * PIECE, PIECE), :]
-    for step in range(1, NY):
-        wait(rsb.at[step - 1], f"r{step}")
-        total = total + rsb[step - 1].astype(F32)
-    here = fown.at[pl.ds(y * PIECE, PIECE), :]
-    here[...] = total.astype(BF16)
-    for step in range(1, NY):
-        send(here, here, {"tm": at_y(step) * 2 + c}, f"g{step}")
-    send(here, foth.at[pl.ds(y * PIECE, PIECE), :], partner, "h0")
-    for step in range(1, NY):
-        rows = pl.ds(at_y(-step) * PIECE, PIECE)
-        wait(fown.at[rows, :], f"g{step}")
-        send(fown.at[rows, :], foth.at[rows, :], partner, f"h{step}")
-    for step in range(NY):
-        wait(foth.at[pl.ds(at_y(-step) * PIECE, PIECE), :], f"h{step}")
+    for number, (band, bands, _) in enumerate(CHUNKS):
+        columns = pl.ds(band * 128, bands * 128)
+
+        @pl.when(c != 0)
+        def _():
+            operand_here(f"m{number}", lambda source: bbuf.at[source, :, columns])
+
+        grad = jnp.zeros((SHARD, bands * 128), F32)
+        for pair in range(NX):
+            rows = jnp.concatenate([abuf[2 * pair], abuf[2 * pair + 1]], axis=1)
+            inner = jnp.concatenate([bbuf[2 * pair, :, columns], bbuf[2 * pair + 1, :, columns]], axis=0)
+            grad = grad + dot(rows, inner, ((1,), (0,)))
+        for at in range(bands):
+            stripe = grad[:, at * 128 : (at + 1) * 128]
+            low = (band + at) * SHARD
+            g32[low : low + SHARD, :] = stripe
+            gs[low : low + SHARD, :] = stripe.astype(BF16)
+        for step in (1, 7, 2, 6, 3, 5, 4):
+            to = at_y(step)
+            send(
+                gs.at[eighth(number, to), :],
+                landing(number, step),
+                {"tm": to * 2 + c},
+                f"r{number}{step}",
+            )
+
+    for number in range(len(CHUNKS)):
+        total = g32[eighth(number, y), :]
+        for step in range(1, NY):
+            wait(landing(number, step), f"r{number}{step}")
+            total = total + landing(number, step)[...].astype(F32)
+        here = fown.at[eighth(number, y), :]
+        here[...] = total.astype(BF16)
+        for step in (1, 7, 2, 6, 3, 5, 4):
+            send(here, here, {"tm": at_y(step) * 2 + c}, f"g{number}{step}")
+        send(here, foth.at[eighth(number, y), :], partner, f"h{number}0")
+    for number in range(len(CHUNKS)):
+        for step in (1, 7, 2, 6, 3, 5, 4):
+            rows = eighth(number, at_y(-step))
+            wait(fown.at[rows, :], f"g{number}{step}")
+            send(fown.at[rows, :], foth.at[rows, :], partner, f"h{number}{step}")
+    for number in range(len(CHUNKS)):
+        for step in range(NY):
+            wait(foth.at[eighth(number, at_y(-step)), :], f"h{number}{step}")
 
     def unstack(source, out):
         for band in range(HIDDEN // 128):
@@ -439,9 +582,9 @@
 
     for copy in sent:
         if isinstance(copy, tuple):
-            role, copy = copy
-
-            @pl.when(c != role)
+            started, copy = copy
+
+            @pl.when(started)
             def _():
                 copy.wait_send()
         else:
@@ -459,9 +602,10 @@
             jax.ShapeDtypeStruct((SHARD, HIDDEN), BF16),
             jax.ShapeDtypeStruct((SHARD, HIDDEN), BF16),
         ),
-        in_specs=[vmem, vmem, vmem, vmem, hbm, hbm, hbm],
+        in_specs=[hbm, vmem, vmem, vmem, hbm, hbm, hbm],
         out_specs=(vmem, vmem, vmem),
         scratch_shapes=[
+            pltpu.VMEM((FRAMES, D), BF16),
             pltpu.VMEM((NX, 3 * CHANNELS, SHARD), BF16),
             pltpu.VMEM((D, HIDDEN), BF16),
             pltpu.VMEM((D, HIDDEN), BF16),
@@ -482,18 +626,18 @@
             pltpu.VMEM((NY - 1, PIECE, 128), BF16),
             pltpu.VMEM((STACK, 128), BF16),
             pltpu.VMEM((STACK, 128), BF16),
-            pltpu.SemaphoreType.DMA((3,)),
-            pltpu.SemaphoreType.DMA((192,)),
-            pltpu.SemaphoreType.DMA((160,)),
+            pltpu.SemaphoreType.DMA((5,)),
+            pltpu.SemaphoreType.DMA((256,)),
+            pltpu.SemaphoreType.DMA((256,)),
         ],
         compiler_params=pltpu.CompilerParams(
-            collective_id=0, has_side_effects=True, vmem_limit_bytes=48 * 1024 * 1024
+            collective_id=0, has_side_effects=True, vmem_limit_bytes=60 * 1024 * 1024
         ),
     )(
         frames[0],
         masked,
         kept_counts,
-        student_gain[None],
+        student_gain,
         wt,
         w_up,
         w_down,

time: 118 us -> 106 us (0.90)
  the two profiles are of different devices: /device:TPU:1 before, /device:TPU:10 now
where the time goes in v2:
time: 106 us
  Pallas kernels  101 us (95%)
  other arithmetic  2.94 us (3%)
  between operations  1.3 us (1%)
    pallas_call x1, Pallas kernels, local(): pl.pallas_call(kernel, out_shape=(jax.ShapeDtypeStruct((CHANNELS, FRAMES)...  101 us
    convert_element_type x2, other arithmetic, local(): return (target.T[None], gup.astype(F32), gdown.astype(F32))  2.94 us

profile of v2, /device:TPU:10, one launch (start us, length us, event | category | flops | bytes accessed | tf_op | source)
XLA Modules:
  0.0 105.8 jit_solution(9321716977086656041)
XLA Ops:
  1.3 100.9 %shard_map.94 = (bf16[160,256]{1,0:T(8,128)(2,1)}, bf16[320,640]{1,0:T(8,128)(2,1)}, bf16[320,640]{1,0:T(8,128)(2,1)}) custom-call(bf16[256,1280]{1,0:T(8,128)(2,1)} %bitcast.7, s32[1,256]{1,0:T(1,128)} %masked_ref.1, s32[1,1]{1,0:T(1,128)S(6)} %copy.11.counts_ref, f32[1280]{0:T(1024)} %gain_ref.1, bf16[480,320]{1,0:T(8,128)(2,1)} %bitcast.8, ...), custom_call_target="tpu_custom_call" | custom-call | tf_op jit(solution)/shard_map/pallas_call | solution.py:598
  102.2 0.0 copy-start
  102.2 2.0 %convert_element_type.6 = f32[320,640]{1,0:T(8,128)} convert(bf16[320,640]{1,0:T(8,128)(2,1)} %get-tuple-element.7) | non-fusion elementwise | flops 204800 | bytes 1228800 | tf_op jit(solution)/shard_map/convert_element_type | solution.py:645
  104.2 0.0 copy-done
  104.2 0.0 copy-start.1
  104.2 0.9 convert_element_type.7
  105.2 0.0 copy-done.1
  105.2 0.6 copy.12
Async XLA Ops:
  102.2 2.0 %copy-start = (bf16[320,640]{1,0:T(8,128)(2,1)S(1)}, bf16[320,640]{1,0:T(8,128)(2,1)}, u32[]{:S(2)}) copy-start(bf16[320,640]{1,0:T(8,128)(2,1)} %get-tuple-element.8) | copy-start | bytes 1228804
  104.2 0.9 copy-start.1

commit v3 on v2

--- a/solution.py
+++ b/solution.py
@@ -127,6 +127,20 @@
         copy.start()
         sent.append(copy)
 
+    done = [0]
+
+    def drain():
+        for copy in sent[done[0] :]:
+            if isinstance(copy, tuple):
+                started, copy = copy
+
+                @pl.when(started)
+                def _():
+                    copy.wait_send()
+            else:
+                copy.wait_send()
+        done[0] = len(sent)
+
     def wait(dst, name):
         describe(dst, dst, partner, names(name), 0).wait_recv()
 
@@ -357,41 +371,28 @@
     attend([(at_y(-1), c), (at_y(1), c)])
     shared(1)
     attend([(at_y(-1), other), (at_y(1), other)])
+    upward.relay()
     forward(2)
-    upward.relay()
     attend([(at_y(-2), c), (at_y(2), c)])
     shared(2)
     attend([(at_y(-2), other), (at_y(2), other)])
+    downward.relay()
     forward(3)
-    downward.relay()
+    upward.share()
     attend([(at_y(-3), c), (at_y(3), c)])
-    upward.share()
-    shared(3)
-    attend([(at_y(-3), other), (at_y(3), other)])
-    forward(4)
-    attend([(at_y(4), c)])
-    shared(4)
-    attend([(at_y(4), other)])
-
-    context = [accum[h][:HEAD] / accum[h][HEAD : HEAD + 1] for h in range(2)]
-    lane = lax.broadcasted_iota(jnp.int32, (HEAD, 128), 1)
-    columns = jnp.zeros((HEAD, 128), F32)
-    for h in range(2):
-        first = jnp.sum(context[h], axis=1, keepdims=True)
-        second = jnp.sum(context[h] * context[h], axis=1, keepdims=True)
-        columns = jnp.where(lane == h, first, jnp.where(lane == 2 + h, second, columns))
-    columns = jnp.concatenate([columns, jnp.zeros((128 - HEAD, 128), F32)], axis=0)
-    stats[0] = columns.T[0:8]
-    for step in range(1, NT):
-        send(stats.at[0], stats.at[step], {"tm": lax.rem(t + step, NT)}, f"s{step}")
-
-    downward.share()
+
     upward.near()
     upward.far()
     pre = dot(normed_ref[...], upbuf[...], ((1,), (0,)))
     cumulative = 0.5 * (1.0 + lax.erf(pre * math.sqrt(0.5)))
     act_ref[...] = (pre * cumulative).astype(BF16)
     slope_ref[...] = cumulative + pre * (jnp.exp(-0.5 * pre * pre) * (1.0 / math.sqrt(2 * math.pi)))
+
+    operand("act", 0, lambda to: act_ref, whole_b)
+    shared(3)
+    attend([(at_y(-3), other), (at_y(3), other)])
+    forward(4)
+    attend([(at_y(4), c)])
 
     def predict(shard, step):
         rows = pl.ds(shard * SHARD, SHARD)
@@ -414,13 +415,29 @@
 
     for step in range(NZ):
         names(f"p{step}")
+    downward.share()
     downward.near()
     for step in (0, 1, 3):
         predict(at_x(step), step)
+    shared(4)
+    attend([(at_y(4), other)])
+
+    context = [accum[h][:HEAD] / accum[h][HEAD : HEAD + 1] for h in range(2)]
+    lane = lax.broadcasted_iota(jnp.int32, (HEAD, 128), 1)
+    columns = jnp.zeros((HEAD, 128), F32)
+    for h in range(2):
+        first = jnp.sum(context[h], axis=1, keepdims=True)
+        second = jnp.sum(context[h] * context[h], axis=1, keepdims=True)
+        columns = jnp.where(lane == h, first, jnp.where(lane == 2 + h, second, columns))
+    columns = jnp.concatenate([columns, jnp.zeros((128 - HEAD, 128), F32)], axis=0)
+    stats[0] = columns.T[0:8]
+    for step in range(1, NT):
+        send(stats.at[0], stats.at[step], {"tm": lax.rem(t + step, NT)}, f"s{step}")
     downward.far()
     predict(at_x(2), 2)
-    operand("act", 0, lambda to: act_ref, whole_b)
     operand("nrm", 1, lambda to: normed_t.at[pl.ds(to * SHARD, SHARD), :], whole_a)
+    drain()
+
 
     total = stats[0]
     for step in range(1, NT):
@@ -478,6 +495,7 @@
 
     pass_on(z)
     back = back_from(z)
+    drain()
     for step in (1, 7, 2, 6, 3, 5, 4):
         owner = at_z(-step)
         wait(cot.at[pl.ds(owner * CHANNELS, CHANNELS), :], f"c{step}")
@@ -489,9 +507,10 @@
         operand(
             f"m{number}",
             1,
-            lambda to: dpre_ref.at[:, columns],
-            lambda source: bbuf.at[source, :, columns],
+            lambda to, columns=columns: dpre_ref.at[:, columns],
+            lambda source, columns=columns: bbuf.at[source, :, columns],
         )
+    drain()
 
     @pl.when(c == 0)
     def _():
@@ -514,14 +533,18 @@
         band, _, rows = CHUNKS[number]
         return pl.ds(band * SHARD + which * rows, rows)
 
-    def landing(number, step):
+    def landing(number, slot):
         band, _, rows = CHUNKS[number]
-        return rsb.at[step - 1, pl.ds(band * SHARD // NY, rows), :]
-
-    rest = STACK - SHARD * HIDDEN // 128
-    g32[STACK - rest :, :] = jnp.zeros((rest, 128), F32)
-    gs[STACK - rest :, :] = jnp.zeros((rest, 128), BF16)
-    for number, (band, bands, _) in enumerate(CHUNKS):
+        return rsb.at[slot, pl.ds(band * SHARD // NY, rows), :]
+
+    def on_y(step):
+        return {"tm": at_y(step) * 2 + c}
+
+    even = lax.rem(y, 2) == 0
+    side = 1 - 2 * lax.rem(y, 2)
+
+    def reduce_first(number):
+        band, bands, _ = CHUNKS[number]
         columns = pl.ds(band * 128, bands * 128)
 
         @pl.when(c != 0)
@@ -538,32 +561,81 @@
             low = (band + at) * SHARD
             g32[low : low + SHARD, :] = stripe
             gs[low : low + SHARD, :] = stripe.astype(BF16)
-        for step in (1, 7, 2, 6, 3, 5, 4):
-            to = at_y(step)
-            send(
-                gs.at[eighth(number, to), :],
-                landing(number, step),
-                {"tm": to * 2 + c},
-                f"r{number}{step}",
-            )
-
-    for number in range(len(CHUNKS)):
+        for slot, step, piece in (
+            (0, 1, at_y(3)),
+            (1, -1, at_y(-3)),
+            (2, 2 * side, at_y(4)),
+            (3, 1, at_y(1)),
+            (4, -1, at_y(-1)),
+        ):
+            send(gs.at[eighth(number, piece), :], landing(number, slot), on_y(step), f"r{number}{slot}")
+
+    def reduce_second(number):
+        for slot in range(3):
+            wait(landing(number, slot), f"r{number}{slot}")
+        far = landing(number, 2)[...].astype(F32)
+        for slot, step, mine in ((5, 2, even), (6, -2, jnp.logical_not(even))):
+            total = g32[eighth(number, at_y(step)), :] + landing(number, slot - 5)[...].astype(F32)
+            total = total + jnp.where(mine, far, 0.0)
+            out = landing(number, slot - 5 + 7)
+            out[...] = total.astype(BF16)
+            send(out, landing(number, slot), on_y(step), f"r{number}{slot}")
+
+    def reduce_last(number):
         total = g32[eighth(number, y), :]
-        for step in range(1, NY):
-            wait(landing(number, step), f"r{number}{step}")
-            total = total + landing(number, step)[...].astype(F32)
+        for slot in (3, 4, 5, 6):
+            wait(landing(number, slot), f"r{number}{slot}")
+            total = total + landing(number, slot)[...].astype(F32)
         here = fown.at[eighth(number, y), :]
         here[...] = total.astype(BF16)
-        for step in (1, 7, 2, 6, 3, 5, 4):
-            send(here, here, {"tm": at_y(step) * 2 + c}, f"g{number}{step}")
+        for step in (2, -2, 1, -1):
+            send(here, here, on_y(step), f"g{number}{step}")
         send(here, foth.at[eighth(number, y), :], partner, f"h{number}0")
+
+    def gathered(number, step):
+        rows = eighth(number, at_y(-step))
+        wait(fown.at[rows, :], f"g{number}{step}")
+        return rows
+
+    def hand_over(number, step, rows):
+        send(fown.at[rows, :], foth.at[rows, :], partner, f"h{number}{step}")
+
+    def gather_first(number):
+        for step in (2, -2):
+            rows = gathered(number, step)
+            near = 1 if step > 0 else -1
+            send(fown.at[rows, :], fown.at[rows, :], on_y(near), f"g{number}{3 * near}")
+            hand_over(number, step, rows)
+        rows = eighth(number, at_y(-2 * side))
+        send(fown.at[rows, :], fown.at[rows, :], on_y(2 * side), f"g{number}4")
+        for step in (1, -1):
+            hand_over(number, step, gathered(number, step))
+
+    def gather_last(number):
+        for step in (3, -3, 4):
+            hand_over(number, step, gathered(number, step))
+
+    rest = STACK - SHARD * HIDDEN // 128
+    g32[STACK - rest :, :] = jnp.zeros((rest, 128), F32)
+    gs[STACK - rest :, :] = jnp.zeros((rest, 128), BF16)
+    reduce_first(0)
+    reduce_first(1)
+    reduce_second(0)
+    reduce_first(2)
+    reduce_second(1)
+    reduce_last(0)
+    reduce_second(2)
+    reduce_last(1)
+    gather_first(0)
+    reduce_last(2)
+    gather_first(1)
+    gather_last(0)
+    gather_first(2)
+    gather_last(1)
+    gather_last(2)
+    drain()
     for number in range(len(CHUNKS)):
-        for step in (1, 7, 2, 6, 3, 5, 4):
-            rows = eighth(number, at_y(-step))
-            wait(fown.at[rows, :], f"g{number}{step}")
-            send(fown.at[rows, :], foth.at[rows, :], partner, f"h{number}{step}")
-    for number in range(len(CHUNKS)):
-        for step in range(NY):
+        for step in (0, 1, -1, 2, -2, 3, -3, 4):
             wait(foth.at[eighth(number, at_y(-step)), :], f"h{number}{step}")
 
     def unstack(source, out):
@@ -580,15 +652,13 @@
         unstack(fown, gup_ref)
         unstack(foth, gdown_ref)
 
-    for copy in sent:
-        if isinstance(copy, tuple):
-            started, copy = copy
-
-            @pl.when(started)
-            def _():
-                copy.wait_send()
-        else:
-            copy.wait_send()
+    drain()
+
+
+def widen(target_ref, gup_ref, gdown_ref, target_out, gup_out, gdown_out):
+    target_out[...] = target_ref[...]
+    gup_out[...] = gup_ref[...].astype(F32)
+    gdown_out[...] = gdown_ref[...].astype(F32)
 
 
 def local(frames, masked, kept_counts, teacher_qkv, student_gain, w_up, w_down):
@@ -623,7 +693,7 @@
             pltpu.VMEM((2 * NX, SLOTS, HIDDEN), BF16),
             pltpu.VMEM((STACK, 128), F32),
             pltpu.VMEM((STACK, 128), BF16),
-            pltpu.VMEM((NY - 1, PIECE, 128), BF16),
+            pltpu.VMEM((NY + 1, PIECE, 128), BF16),
             pltpu.VMEM((STACK, 128), BF16),
             pltpu.VMEM((STACK, 128), BF16),
             pltpu.SemaphoreType.DMA((5,)),
@@ -642,7 +712,17 @@
         w_up,
         w_down,
     )
-    return target.T[None], gup.astype(F32), gdown.astype(F32)
+    target, gup, gdown = pl.pallas_call(
+        widen,
+        out_shape=(
+            jax.ShapeDtypeStruct((CHANNELS, FRAMES), BF16),
+            jax.ShapeDtypeStruct((SHARD, HIDDEN), F32),
+            jax.ShapeDtypeStruct((SHARD, HIDDEN), F32),
+        ),
+        in_specs=[vmem] * 3,
+        out_specs=(vmem, vmem, vmem),
+    )(target, gup, gdown)
+    return target.T[None], gup, gdown
 
 
 def solution(mesh):

time: 106 us -> 106 us (level)
  the two profiles are of different devices: /device:TPU:10 before, /device:TPU:1 now
where the time goes in v3:
time: 106 us
  Pallas kernels  105 us (99%)
  between operations  1.29 us (1%)
    pallas_call x1, Pallas kernels, local(): pl.pallas_call(kernel, out_shape=(jax.ShapeDtypeStruct((CHANNELS, FRAMES)...  103 us
    pallas_call x1, Pallas kernels, local(): pl.pallas_call(widen, out_shape=(jax.ShapeDtypeStruct((CHANNELS, FRAMES),...  2.4 us

profile of v3, /device:TPU:1, one launch (start us, length us, event | category | flops | bytes accessed | tf_op | source)
XLA Modules:
  0.0 106.3 jit_solution(735257949739702667)
XLA Ops:
  1.3 102.6 %shard_map.94 = (bf16[160,256]{1,0:T(8,128)(2,1)}, bf16[320,640]{1,0:T(8,128)(2,1)}, bf16[320,640]{1,0:T(8,128)(2,1)}) custom-call(bf16[256,1280]{1,0:T(8,128)(2,1)} %bitcast.7, s32[1,256]{1,0:T(1,128)} %masked_ref.1, s32[1,1]{1,0:T(1,128)S(6)} %copy.10.counts_ref, f32[1280]{0:T(1024)} %gain_ref.1, bf16[480,320]{1,0:T(8,128)(2,1)} %bitcast.8, ...), custom_call_target="tpu_custom_call" | custom-call | tf_op jit(solution)/shard_map/pallas_call | solution.py:668
  103.9 2.4 %shard_map.95 = (bf16[160,256]{1,0:T(8,128)(2,1)}, f32[320,640]{1,0:T(8,128)}, f32[320,640]{1,0:T(8,128)}) custom-call(bf16[160,256]{1,0:T(8,128)(2,1)} %get-tuple-element.9.target_ref, bf16[320,640]{1,0:T(8,128)(2,1)} %get-tuple-element.10.gup_ref, bf16[320,640]{1,0:T(8,128)(2,1)} %get-tuple-element.11.gdown_ref), custom_call_target="tpu_custom_call" | custom-call | tf_op jit(solution)/shard_map/pallas_call | solution.py:715

commit v4 on v3

--- a/solution.py
+++ b/solution.py
@@ -22,8 +22,10 @@
 NT = 2 * NY
 PIECE = 208
 STACK = NY * PIECE
-CHUNKS = ((0, 2, 80), (2, 2, 80), (4, 1, 48))
+CHUNKS = ((0, 2, 80), (2, 3, 128))
 NEAR = (1, 3, 2)
+SENDS, RECEIVES = 13, 67
+METER = 5120
 LENGTH = NT * FRAMES
 SCALE = HEAD**-0.5
 
@@ -72,6 +74,7 @@
     rsb,
     fown,
     foth,
+    meter,
     local_sem,
     send_sem,
     recv_sem,
@@ -109,40 +112,35 @@
         pl.semaphore_signal(barrier, inc=1, device_id=peer, device_id_type=MESH)
     pl.semaphore_wait(barrier, len(peers))
 
-    names = Names()
-    sent = []
-
-    def describe(src, dst, device, name, out):
+    names, outs = Names(), Names()
+    left_here = {}
+
+    def describe(src, dst, device, name, group):
         return pltpu.make_async_remote_copy(
             src_ref=src,
             dst_ref=dst,
-            send_sem=send_sem.at[out],
-            recv_sem=recv_sem.at[name],
+            send_sem=send_sem.at[outs(group)],
+            recv_sem=recv_sem.at[names(name)],
             device_id=device,
             device_id_type=MESH,
         )
 
-    def send(src, dst, device, name):
-        copy = describe(src, dst, device, names(name), len(sent))
-        copy.start()
-        sent.append(copy)
-
-    done = [0]
-
-    def drain():
-        for copy in sent[done[0] :]:
-            if isinstance(copy, tuple):
-                started, copy = copy
-
-                @pl.when(started)
-                def _():
-                    copy.wait_send()
-            else:
-                copy.wait_send()
-        done[0] = len(sent)
+    def send(src, dst, device, name, group):
+        describe(src, dst, device, name, group).start()
+        count(src, group)
+
+    def count(src, group):
+        left_here[group] = left_here.get(group, 0) + math.prod(src.shape) * src.dtype.itemsize // 256
 
     def wait(dst, name):
-        describe(dst, dst, partner, names(name), 0).wait_recv()
+        describe(dst, dst, partner, name, "w").wait_recv()
+
+    def pieces(rows):
+        return meter.at[pl.ds(0, rows), :]
+
+    def wait_left(group, refs=None):
+        refs = pieces(left_here[group]) if refs is None else refs
+        describe(refs, refs, partner, "w1", group).wait_send()
 
     def place_w(shard, row, rows):
         return wbuf.at[shard, pl.ds(row, rows), :]
@@ -165,19 +163,18 @@
             mine = self.src.at[pl.ds(self.mine, self.half), :]
             there = self.place(x, self.mine, self.half)
             for step in NEAR:
-                send(mine, there, {"dp": at_x(step)}, f"{self.name}{step}")
+                send(mine, there, {"dp": at_x(step)}, f"{self.name}{step}", "w")
             self.own.start()
 
         def share(self):
             for step in NEAR:
                 block = self.place(at_x(-step), self.mine, self.half)
                 wait(block, f"{self.name}{step}")
-                send(block, block, partner, f"{self.name}P{step}")
+                send(block, block, partner, f"{self.name}P", "w")
 
         def finish(self):
             self.own.wait()
-            for step in NEAR:
-                wait(self.place(at_x(-step), self.theirs, self.half), f"{self.name}P{step}")
+            wait(wbuf.at[pl.ds(0, NX - 1), pl.ds(self.theirs, self.half), :], f"{self.name}P")
 
     class Relay:
         def __init__(self, name, src, place, half, first, sem):
@@ -189,8 +186,8 @@
         def start(self):
             mine = self.src.at[pl.ds(self.mine, self.half), :]
             there = self.place(x, self.mine, self.half)
-            send(mine, there, {"dp": at_x(1)}, self.name + "R0")
-            send(mine, there, {"dp": at_x(-1)}, self.name + "L0")
+            send(mine, there, {"dp": at_x(1)}, self.name + "R0", self.name)
+            send(mine, there, {"dp": at_x(-1)}, self.name + "L0", self.name)
             self.own.start()
 
         def relay(self):
@@ -198,34 +195,30 @@
             block = self.place(at_x(-1), self.mine, n)
             wait(block, self.name + "R0")
             part = self.place(at_x(-1), self.mine, first)
-            send(part, part, {"dp": at_x(1)}, self.name + "R1")
-            send(block, block, partner, self.name + "P0")
+            send(part, part, {"dp": at_x(1)}, self.name + "R1", self.name)
+            send(block, block, partner, self.name + "P0", self.name)
             block = self.place(at_x(1), self.mine, n)
             wait(block, self.name + "L0")
             part = self.place(at_x(1), self.mine + first, n - first)
-            send(part, part, {"dp": at_x(-1)}, self.name + "L1")
-            send(block, block, partner, self.name + "P1")
+            send(part, part, {"dp": at_x(-1)}, self.name + "L1", self.name)
+            send(block, block, partner, self.name + "P0", self.name)
 
         def share(self):
             n, first = self.half, self.first
             far = at_x(2)
             part = self.place(far, self.mine, first)
             wait(part, self.name + "R1")
-            send(part, part, partner, self.name + "P2")
+            send(part, part, partner, self.name + "P2", self.name)
             part = self.place(far, self.mine + first, n - first)
             wait(part, self.name + "L1")
-            send(part, part, partner, self.name + "P3")
+            send(part, part, partner, self.name + "P2", self.name)
 
         def near(self):
-            n = self.half
             self.own.wait()
-            wait(self.place(at_x(-1), self.theirs, n), self.name + "P0")
-            wait(self.place(at_x(1), self.theirs, n), self.name + "P1")
+            wait(self.place(0, 0, 2 * self.half), self.name + "P0")
 
         def far(self):
-            n, first = self.half, self.first
-            wait(self.place(at_x(2), self.theirs, first), self.name + "P2")
-            wait(self.place(at_x(2), self.theirs + first, n - first), self.name + "P3")
+            wait(self.place(at_x(2), self.theirs, self.half), self.name + "P2")
 
     teacher_kv = Direct("w", wt_ref, place_w, CHANNELS, CHANNELS, 0)
     teacher_q = Direct("q", wt_ref, place_w, 0, HEAD, 3)
@@ -269,9 +262,9 @@
     right, left = {"tm": at_y(1) * 2 + c}, {"tm": at_y(-1) * 2 + c}
     for part, tag in ((0, "k"), (1, "v")):
         mine = block(y, c, part)
-        send(mine, mine, right, tag + "R0")
-        send(mine, mine, left, tag + "L0")
-        send(mine, mine, partner, tag + "P0")
+        send(mine, mine, right, tag + "R0", tag)
+        send(mine, mine, left, tag + "L0", tag)
+        send(mine, mine, partner, "s0", tag)
     upward.start()
     teacher_q.share()
     teacher_q.finish()
@@ -306,57 +299,35 @@
                 here = block(behind, c, part)
                 wait(here, f"{tag}R{step - 1}")
                 if step < 3 or (step == 3 and part == 0):
-                    send(here, here, right, f"{tag}R{step}")
-                send(here, here, partner, f"{tag}PR{step}")
+                    send(here, here, right, f"{tag}R{step}", tag)
+                send(here, here, partner, f"s{step}", tag)
             if step < 4 or part == 1:
                 here = block(ahead, c, part)
                 wait(here, f"{tag}L{step - 1}")
                 if step < 3 or (step == 3 and part == 1):
-                    send(here, here, left, f"{tag}L{step}")
-                send(here, here, partner, f"{tag}PL{step}")
+                    send(here, here, left, f"{tag}L{step}", tag)
+                send(here, here, partner, f"s{step}", tag)
 
     def shared(step):
-        for part, tag in ((0, "k"), (1, "v")):
-            if step == 0:
-                wait(block(y, other, part), tag + "P0")
-                continue
-            if step < 4 or part == 0:
-                wait(block(at_y(-step), other, part), f"{tag}PR{step}")
-            if step < 4 or part == 1:
-                wait(block(at_y(step), other, part), f"{tag}PL{step}")
+        wait(kv.at[y, other] if step in (0, 4) else kv.at[y], f"s{step}")
 
     me = x * 2 + c
 
     def operand(tag, role, source, place):
         for step in NEAR:
-            sem = names(f"{tag}{step}0")
-            names(f"{tag}{step}1")
-            copy = describe(
-                source(at_x(step)), place(me), {"dp": at_x(step), "tm": y * 2 + role}, sem + c, len(sent)
-            )
-            copy.start()
-            sent.append(copy)
-        sem = names(f"{tag}00")
-        names(f"{tag}01")
-        copy = describe(source(x), place(me), partner, sem + c, len(sent))
+            send(source(at_x(step)), place(me), {"dp": at_x(step), "tm": y * 2 + role}, tag, "o" + tag[0])
 
         @pl.when(c == role)
         def _():
             place(me)[...] = source(x)[...]
 
+        copy = describe(source(x), place(me), partner, tag, "partner")
+
         @pl.when(c != role)
         def _():
             copy.start()
 
-        sent.append((c != role, copy))
-
-    def operand_here(tag, place):
-        here = place(x * 2 + other)
-        describe(here, here, partner, names(f"{tag}00") + other, 0).wait_recv()
-        for step in NEAR:
-            for core in range(2):
-                here = place(at_x(-step) * 2 + core)
-                describe(here, here, partner, names(f"{tag}{step}{core}"), 0).wait_recv()
+        count(source(x), f"partner{1 - role}")
 
     def whole_a(source):
         return abuf.at[source]
@@ -399,22 +370,13 @@
         psend[rows, :] = dot(downbuf[rows, :], act_ref[...], ((1,), (1,))).astype(BF16)
         for half in range(2):
             to = shard * 2 + half
-            copy = describe(
-                psend.at[pl.ds(to * CHANNELS, CHANNELS), :],
-                precv.at[z],
-                {"head": to},
-                names("p0") + lax.rem(to - z + NZ, NZ),
-                len(sent),
-            )
+            source = psend.at[pl.ds(to * CHANNELS, CHANNELS), :]
+            copy = describe(source, precv.at[lax.rem(to - z + NZ, NZ)], {"head": to}, "p", "p")
 
             @pl.when(to != z)
             def _():
                 copy.start()
 
-            sent.append((to != z, copy))
-
-    for step in range(NZ):
-        names(f"p{step}")
     downward.share()
     downward.near()
     for step in (0, 1, 3):
@@ -432,16 +394,15 @@
     columns = jnp.concatenate([columns, jnp.zeros((128 - HEAD, 128), F32)], axis=0)
     stats[0] = columns.T[0:8]
     for step in range(1, NT):
-        send(stats.at[0], stats.at[step], {"tm": lax.rem(t + step, NT)}, f"s{step}")
+        send(stats.at[0], stats.at[step], {"tm": lax.rem(t + step, NT)}, "stats", "z")
     downward.far()
     predict(at_x(2), 2)
     operand("nrm", 1, lambda to: normed_t.at[pl.ds(to * SHARD, SHARD), :], whole_a)
-    drain()
-
-
+
+
+    wait(stats.at[pl.ds(1, NT - 1)], "stats")
     total = stats[0]
     for step in range(1, NT):
-        wait(stats.at[step], f"s{step}")
         total = total + stats[step]
     columns = jnp.concatenate([total, jnp.zeros((120, 128), F32)], axis=0).T
     parts = []
@@ -453,20 +414,17 @@
     target_ref[...] = target
 
     aim = dot(target, pick, ((1,), (1,)))
+    wait(precv.at[pl.ds(1, NZ - 1)], "p")
     pred = psend[pl.ds(z * CHANNELS, CHANNELS), :].astype(F32)
     for step in range(1, NZ):
-        wait(precv.at[at_z(-step)], f"p{step}")
-        pred = pred + precv[at_z(-step)].astype(F32)
+        pred = pred + precv[step].astype(F32)
     number = lax.broadcasted_iota(jnp.int32, (CHANNELS, SLOTS), 1)
     valid = number < jnp.broadcast_to(counts_ref[...], (CHANNELS, SLOTS))
     gap = jnp.where(valid, pred - aim, 0.0) * (2.0 / math.sqrt(D))
     here = cot.at[pl.ds(z * CHANNELS, CHANNELS), :]
     here[...] = gap.astype(BF16)
     for step in (1, 7, 2, 6, 3, 5, 4):
-        send(here, here, {"head": at_z(step)}, f"c{step}")
-
-    for step in range(4 * NX):
-        names(f"e{step}")
+        send(here, here, {"head": at_z(step)}, f"c{step}", "z")
 
     def half_a(source, half):
         return abuf.at[source, pl.ds(half * CHANNELS, CHANNELS), :]
@@ -474,8 +432,7 @@
     def pass_on(owner):
         to, half = owner // 2, lax.rem(owner, 2)
         source = cot.at[pl.ds(owner * CHANNELS, CHANNELS), :]
-        sem = names("e0") + lax.rem(to - x + NX, NX) * 4 + c * 2 + half
-        copy = describe(source, half_a(me, half), {"dp": to, "tm": y * 2}, sem, len(sent))
+        copy = describe(source, half_a(me, half), {"dp": to, "tm": y * 2}, "e", "e")
         mine = jnp.logical_and(to == x, c == 0)
         away = jnp.logical_not(mine)
 
@@ -487,15 +444,12 @@
         def _():
             copy.start()
 
-        sent.append((away, copy))
-
     def back_from(owner):
         rows = pl.ds(owner * CHANNELS, CHANNELS)
         return dot(cot[rows, :], downbuf[rows, :], ((0,), (0,)))
 
     pass_on(z)
     back = back_from(z)
-    drain()
     for step in (1, 7, 2, 6, 3, 5, 4):
         owner = at_z(-step)
         wait(cot.at[pl.ds(owner * CHANNELS, CHANNELS), :], f"c{step}")
@@ -510,24 +464,15 @@
             lambda to, columns=columns: dpre_ref.at[:, columns],
             lambda source, columns=columns: bbuf.at[source, :, columns],
         )
-    drain()
 
     @pl.when(c == 0)
     def _():
-        operand_here("act", whole_b)
-        for step in (0, *NEAR):
-            for core in range(2):
-                for half in range(2):
-                    here = half_a(at_x(-step) * 2 + core, half)
-                    copy = describe(
-                        here, here, partner, names("e0") + step * 4 + core * 2 + half, 0
-                    )
-                    if (step, core) != (0, 0):
-                        copy.wait_recv()
+        wait(bbuf.at[pl.ds(0, 2 * NX - 1)], "act")
+        wait(abuf.at[pl.ds(0, 2 * NX - 1)], "e")
 
     @pl.when(c != 0)
     def _():
-        operand_here("nrm", whole_a)
+        wait(abuf.at[pl.ds(0, 2 * NX - 1)], "nrm")
 
     def eighth(number, which):
         band, _, rows = CHUNKS[number]
@@ -549,7 +494,7 @@
 
         @pl.when(c != 0)
         def _():
-            operand_here(f"m{number}", lambda source: bbuf.at[source, :, columns])
+            wait(bbuf.at[pl.ds(0, 2 * NX - 1), :, columns], f"m{number}")
 
         grad = jnp.zeros((SHARD, bands * 128), F32)
         for pair in range(NX):
@@ -568,52 +513,55 @@
             (3, 1, at_y(1)),
             (4, -1, at_y(-1)),
         ):
-            send(gs.at[eighth(number, piece), :], landing(number, slot), on_y(step), f"r{number}{slot}")
+            send(
+                gs.at[eighth(number, piece), :],
+                landing(number, slot),
+                on_y(step),
+                f"r{number}{slot // 3}",
+                "y",
+            )
 
     def reduce_second(number):
-        for slot in range(3):
-            wait(landing(number, slot), f"r{number}{slot}")
+        wait(landing(number, pl.ds(0, 3)), f"r{number}0")
         far = landing(number, 2)[...].astype(F32)
         for slot, step, mine in ((5, 2, even), (6, -2, jnp.logical_not(even))):
             total = g32[eighth(number, at_y(step)), :] + landing(number, slot - 5)[...].astype(F32)
             total = total + jnp.where(mine, far, 0.0)
             out = landing(number, slot - 5 + 7)
             out[...] = total.astype(BF16)
-            send(out, landing(number, slot), on_y(step), f"r{number}{slot}")
+            send(out, landing(number, slot), on_y(step), f"r{number}1", "y")
 
     def reduce_last(number):
         total = g32[eighth(number, y), :]
+        wait(landing(number, pl.ds(3, 4)), f"r{number}1")
         for slot in (3, 4, 5, 6):
-            wait(landing(number, slot), f"r{number}{slot}")
             total = total + landing(number, slot)[...].astype(F32)
         here = fown.at[eighth(number, y), :]
         here[...] = total.astype(BF16)
-        for step in (2, -2, 1, -1):
-            send(here, here, on_y(step), f"g{number}{step}")
-        send(here, foth.at[eighth(number, y), :], partner, f"h{number}0")
-
-    def gathered(number, step):
-        rows = eighth(number, at_y(-step))
-        wait(fown.at[rows, :], f"g{number}{step}")
-        return rows
-
-    def hand_over(number, step, rows):
-        send(fown.at[rows, :], foth.at[rows, :], partner, f"h{number}{step}")
+        for step, tag in ((2, "a"), (-2, "b"), (1, "c"), (-1, "c")):
+            send(here, here, on_y(step), f"g{number}{tag}", "y")
+        hand_over(number, eighth(number, y))
+
+    def hand_over(number, rows):
+        send(fown.at[rows, :], foth.at[rows, :], partner, f"h{number}", "y")
 
     def gather_first(number):
-        for step in (2, -2):
-            rows = gathered(number, step)
-            near = 1 if step > 0 else -1
-            send(fown.at[rows, :], fown.at[rows, :], on_y(near), f"g{number}{3 * near}")
-            hand_over(number, step, rows)
+        size = CHUNKS[number][2]
+        for step, tag in ((2, "a"), (-2, "b")):
+            rows = eighth(number, at_y(-step))
+            wait(fown.at[rows, :], f"g{number}{tag}")
+            send(fown.at[rows, :], fown.at[rows, :], on_y(step // 2), f"g{number}d", "y")
+            hand_over(number, rows)
         rows = eighth(number, at_y(-2 * side))
-        send(fown.at[rows, :], fown.at[rows, :], on_y(2 * side), f"g{number}4")
+        send(fown.at[rows, :], fown.at[rows, :], on_y(2 * side), f"g{number}d", "y")
+        wait(pieces(2 * size), f"g{number}c")
         for step in (1, -1):
-            hand_over(number, step, gathered(number, step))
+            hand_over(number, eighth(number, at_y(-step)))
 
     def gather_last(number):
+        wait(pieces(3 * CHUNKS[number][2]), f"g{number}d")
         for step in (3, -3, 4):
-            hand_over(number, step, gathered(number, step))
+            hand_over(number, eighth(number, at_y(-step)))
 
     rest = STACK - SHARD * HIDDEN // 128
     g32[STACK - rest :, :] = jnp.zeros((rest, 128), F32)
@@ -621,22 +569,15 @@
     reduce_first(0)
     reduce_first(1)
     reduce_second(0)
-    reduce_first(2)
     reduce_second(1)
     reduce_last(0)
-    reduce_second(2)
     reduce_last(1)
     gather_first(0)
-    reduce_last(2)
     gather_first(1)
     gather_last(0)
-    gather_first(2)
     gather_last(1)
-    gather_last(2)
-    drain()
-    for number in range(len(CHUNKS)):
-        for step in (0, 1, -1, 2, -2, 3, -3, 4):
-            wait(foth.at[eighth(number, at_y(-step)), :], f"h{number}{step}")
+    for number, (band, _, rows) in enumerate(CHUNKS):
+        wait(foth.at[pl.ds(band * SHARD, NY * rows), :], f"h{number}")
 
     def unstack(source, out):
         for band in range(HIDDEN // 128):
@@ -652,7 +593,22 @@
         unstack(fown, gup_ref)
         unstack(foth, gdown_ref)
 
-    drain()
+    wait_left("w", wbuf.at[pl.ds(0, NX - 1)])
+    wait_left("p", pieces((NZ - 1) * CHANNELS))
+    for group in ("u", "d", "k", "v", "z", "y", "oa", "on", "om"):
+        wait_left(group)
+
+    @pl.when(c == 0)
+    def _():
+        wait_left("partner", pieces(left_here["partner0"]))
+        wait_left("e", pieces((NZ - 2) * CHANNELS))
+
+    @pl.when(c != 0)
+    def _():
+        wait_left("partner", pieces(left_here["partner1"]))
+        wait_left("e", pieces(NZ * CHANNELS))
+
+    assert len(names.index) <= RECEIVES and len(outs.index) <= SENDS
 
 
 def widen(target_ref, gup_ref, gdown_ref, target_out, gup_out, gdown_out):
@@ -664,7 +620,7 @@
 def local(frames, masked, kept_counts, teacher_qkv, student_gain, w_up, w_down):
     wt = teacher_qkv.transpose(1, 2, 0).reshape(3 * CHANNELS, SHARD)
     vmem = pl.BlockSpec(memory_space=pltpu.VMEM)
-    hbm = pl.BlockSpec(memory_space=pl.ANY)
+    hbm = pl.BlockSpec(memory_space=pltpu.HBM)
     target, gup, gdown = pl.pallas_call(
         kernel,
         out_shape=(
@@ -696,12 +652,13 @@
             pltpu.VMEM((NY + 1, PIECE, 128), BF16),
             pltpu.VMEM((STACK, 128), BF16),
             pltpu.VMEM((STACK, 128), BF16),
+            pltpu.VMEM((METER, 128), BF16),
             pltpu.SemaphoreType.DMA((5,)),
-            pltpu.SemaphoreType.DMA((256,)),
-            pltpu.SemaphoreType.DMA((256,)),
+            pltpu.SemaphoreType.DMA((SENDS,)),
+            pltpu.SemaphoreType.DMA((RECEIVES,)),
         ],
         compiler_params=pltpu.CompilerParams(
-            collective_id=0, has_side_effects=True, vmem_limit_bytes=60 * 1024 * 1024
+            collective_id=0, has_side_effects=True, vmem_limit_bytes=32 * 1024 * 1024
         ),
     )(
         frames[0],

time: 106 us -> 103 us (0.972); the launches traced: 106 us -> 102 us
  Pallas kernels: 105 us -> 92.8 us
  local copies, waits for them, and re-layouts: 0 us -> 7.56 us
    pallas_call x1, Pallas kernels: 103 us -> 90.4 us  [local(): pl.pallas_call(kernel, out_shape=(jax.ShapeDtypeStruct((CHANNELS, FRAMES)...]
    unnamed x0 -> x18, local copies, waits for them, and re-layouts: none -> 7.56 us
where the time goes in v4:
time: 103 us; the launch traced here: 102 us
  Pallas kernels  92.8 us (90%)
  local copies, waits for them, and re-layouts  7.56 us (7%)
  between operations  1.31 us (1%)
    pallas_call x1, Pallas kernels, local(): pl.pallas_call(kernel, out_shape=(jax.ShapeDtypeStruct((CHANNELS, FRAMES)...  90.4 us
    unnamed x18, local copies, waits for them, and re-layouts  7.56 us
    pallas_call x1, Pallas kernels, local(): pl.pallas_call(widen, out_shape=(jax.ShapeDtypeStruct((CHANNELS, FRAMES),...  2.4 us

profile of v4, /device:TPU:1, one launch (start us, length us, event | category | flops | bytes accessed | tf_op | source)
XLA Modules:
  0.0 101.7 jit_solution(17214381427909017424)
XLA Ops:
  1.3 0.0 copy-start.8
  1.3 0.7 copy-done.8
  2.0 0.0 copy-start
  2.0 1.1 %copy-done = bf16[1,256,1280]{2,1,0:T(8,128)(2,1)S(1)} copy-done((bf16[1,256,1280]{2,1,0:T(8,128)(2,1)S(1)}, bf16[1,256,1280]{2,1,0:T(8,128)(2,1)}, u32[]{:S(2)}) %copy-start) | copy-done | bytes 655384
  3.0 0.0 copy-start.3
  3.0 1.0 copy-done.3
  4.0 0.0 copy-start.4
  4.0 1.0 copy-done.4
  5.0 0.0 copy-start.5
  5.1 1.0 copy-done.5
  6.0 0.0 copy-start.7
  6.0 0.7 copy-done.7
  6.7 90.4 %shard_map.94 = (bf16[160,256]{1,0:T(8,128)(2,1)S(1)}, bf16[320,640]{1,0:T(8,128)(2,1)S(1)}, bf16[320,640]{1,0:T(8,128)(2,1)S(1)}) custom-call(bf16[256,1280]{1,0:T(8,128)(2,1)S(1)} %bitcast.7, s32[1,256]{1,0:T(1,128)S(1)} %copy-done.8, s32[1,1]{1,0:T(1,128)S(6)} %copy.10.counts_ref, f32[1280]{0:T(1024)S(1)} %copy-done.7, bf16[480,320]{1,0:T(8,128)(2,1)S(1)} %bitcast.8, ...), custom_call_target="tpu_custom_call" | custom-call | tf_op jit(solution)/shard_map/pallas_call | solution.py:624
  97.1 0.0 copy-start.1
  97.1 0.7 copy-done.1
  97.9 0.0 copy-start.2
  97.9 0.7 copy-done.2
  98.6 0.0 copy-start.6
  98.6 0.6 copy-done.6
  99.3 2.4 %shard_map.95 = (bf16[160,256]{1,0:T(8,128)(2,1)}, f32[320,640]{1,0:T(8,128)}, f32[320,640]{1,0:T(8,128)}) custom-call(bf16[160,256]{1,0:T(8,128)(2,1)} %copy-done.6, bf16[320,640]{1,0:T(8,128)(2,1)} %copy-done.1, bf16[320,640]{1,0:T(8,128)(2,1)} %copy-done.2), custom_call_target="tpu_custom_call" | custom-call | tf_op jit(solution)/shard_map/pallas_call | solution.py:672
Async XLA Ops:
  1.3 0.7 copy-start.8
  2.0 1.1 %copy-start = (bf16[1,256,1280]{2,1,0:T(8,128)(2,1)S(1)}, bf16[1,256,1280]{2,1,0:T(8,128)(2,1)}, u32[]{:S(2)}) copy-start(bf16[1,256,1280]{2,1,0:T(8,128)(2,1)} %param.7) | copy-start | bytes 1966084
  3.0 1.0 copy-start.3
  4.0 1.0 copy-start.4
  5.0 1.0 copy-start.5
  6.0 0.7 copy-start.7
  97.1 0.7 copy-start.1
  97.9 0.7 copy-start.2
  98.6 0.6 copy-start.6

commit v5 on v4

--- a/solution.py
+++ b/solution.py
@@ -226,6 +226,7 @@
     downward = Relay("d", down_ref, place_down, 160, 80, 2)
 
     teacher_kv.start()
+    teacher_q.start()
 
     keep = 1 - masked_ref[...]
     keep = keep.astype(F32)
@@ -256,7 +257,8 @@
         return kv.at[source, core, pl.ds(part * CHANNELS, CHANNELS), :]
 
     teacher_kv.share()
-    teacher_q.start()
+    upward.start()
+    downward.start()
     teacher_kv.finish()
     kv[y, c] = project(CHANNELS, 3 * CHANNELS)
     right, left = {"tm": at_y(1) * 2 + c}, {"tm": at_y(-1) * 2 + c}
@@ -265,10 +267,8 @@
         send(mine, mine, right, tag + "R0", tag)
         send(mine, mine, left, tag + "L0", tag)
         send(mine, mine, partner, "s0", tag)
-    upward.start()
     teacher_q.share()
     teacher_q.finish()
-    downward.start()
     query = project(0, CHANNELS)
     query = [query[h * HEAD : (h + 1) * HEAD] for h in range(2)]
 
@@ -338,33 +338,6 @@
     attend([(y, c)])
     shared(0)
     attend([(y, other)])
-    forward(1)
-    attend([(at_y(-1), c), (at_y(1), c)])
-    shared(1)
-    attend([(at_y(-1), other), (at_y(1), other)])
-    upward.relay()
-    forward(2)
-    attend([(at_y(-2), c), (at_y(2), c)])
-    shared(2)
-    attend([(at_y(-2), other), (at_y(2), other)])
-    downward.relay()
-    forward(3)
-    upward.share()
-    attend([(at_y(-3), c), (at_y(3), c)])
-
-    upward.near()
-    upward.far()
-    pre = dot(normed_ref[...], upbuf[...], ((1,), (0,)))
-    cumulative = 0.5 * (1.0 + lax.erf(pre * math.sqrt(0.5)))
-    act_ref[...] = (pre * cumulative).astype(BF16)
-    slope_ref[...] = cumulative + pre * (jnp.exp(-0.5 * pre * pre) * (1.0 / math.sqrt(2 * math.pi)))
-
-    operand("act", 0, lambda to: act_ref, whole_b)
-    shared(3)
-    attend([(at_y(-3), other), (at_y(3), other)])
-    forward(4)
-    attend([(at_y(4), c)])
-
     def predict(shard, step):
         rows = pl.ds(shard * SHARD, SHARD)
         psend[rows, :] = dot(downbuf[rows, :], act_ref[...], ((1,), (1,))).astype(BF16)
@@ -377,10 +350,39 @@
             def _():
                 copy.start()
 
+    forward(1)
+    upward.relay()
+    attend([(at_y(-1), c), (at_y(1), c)])
+    shared(1)
+    attend([(at_y(-1), other), (at_y(1), other)])
+    downward.relay()
+    forward(2)
+    attend([(at_y(-2), c), (at_y(2), c)])
+    shared(2)
+    attend([(at_y(-2), other), (at_y(2), other)])
+    upward.share()
+    forward(3)
+    attend([(at_y(-3), c), (at_y(3), c)])
+
+    upward.near()
+    upward.far()
+    pre = dot(normed_ref[...], upbuf[...], ((1,), (0,)))
+    cumulative = 0.5 * (1.0 + lax.erf(pre * math.sqrt(0.5)))
+    act_ref[...] = (pre * cumulative).astype(BF16)
+    slope_ref[...] = cumulative + pre * (jnp.exp(-0.5 * pre * pre) * (1.0 / math.sqrt(2 * math.pi)))
+
+    operand("act", 0, lambda to: act_ref, whole_b)
+    shared(3)
+    attend([(at_y(-3), other), (at_y(3), other)])
     downward.share()
+    forward(4)
+
     downward.near()
     for step in (0, 1, 3):
         predict(at_x(step), step)
+    attend([(at_y(4), c)])
+    downward.far()
+    predict(at_x(2), 2)
     shared(4)
     attend([(at_y(4), other)])
 
@@ -395,36 +397,39 @@
     stats[0] = columns.T[0:8]
     for step in range(1, NT):
         send(stats.at[0], stats.at[step], {"tm": lax.rem(t + step, NT)}, "stats", "z")
-    downward.far()
-    predict(at_x(2), 2)
-    operand("nrm", 1, lambda to: normed_t.at[pl.ds(to * SHARD, SHARD), :], whole_a)
-
+
+
+    wait(precv.at[pl.ds(1, NZ - 1)], "p")
+    pred = psend[pl.ds(z * CHANNELS, CHANNELS), :].astype(F32)
+    for step in range(1, NZ):
+        pred = pred + precv[step].astype(F32)
+    context = jnp.concatenate(context, axis=0)
+    centre = jnp.mean(context, axis=1, keepdims=True)
+    raw = dot((context - centre).astype(BF16), pick, ((1,), (1,)))
+    number = lax.broadcasted_iota(jnp.int32, (CHANNELS, SLOTS), 1)
+    valid = number < jnp.broadcast_to(counts_ref[...], (CHANNELS, SLOTS))
 
     wait(stats.at[pl.ds(1, NT - 1)], "stats")
     total = stats[0]
     for step in range(1, NT):
         total = total + stats[step]
     columns = jnp.concatenate([total, jnp.zeros((120, 128), F32)], axis=0).T
-    parts = []
+    means, scales = [], []
     for h in range(2):
         mean = columns[:HEAD, h : h + 1] * (1.0 / LENGTH)
         var = columns[:HEAD, 2 + h : 3 + h] * (1.0 / LENGTH) - mean * mean
-        parts.append((context[h] - mean) * lax.rsqrt(var + 1e-5))
-    target = jnp.concatenate(parts, axis=0).astype(BF16)
-    target_ref[...] = target
-
-    aim = dot(target, pick, ((1,), (1,)))
-    wait(precv.at[pl.ds(1, NZ - 1)], "p")
-    pred = psend[pl.ds(z * CHANNELS, CHANNELS), :].astype(F32)
-    for step in range(1, NZ):
-        pred = pred + precv[step].astype(F32)
-    number = lax.broadcasted_iota(jnp.int32, (CHANNELS, SLOTS), 1)
-    valid = number < jnp.broadcast_to(counts_ref[...], (CHANNELS, SLOTS))
+        means.append(mean)
+        scales.append(lax.rsqrt(var + 1e-5))
+    mean, scale = jnp.concatenate(means, axis=0), jnp.concatenate(scales, axis=0)
+
+    aim = (raw + (centre - mean)) * scale
     gap = jnp.where(valid, pred - aim, 0.0) * (2.0 / math.sqrt(D))
     here = cot.at[pl.ds(z * CHANNELS, CHANNELS), :]
     here[...] = gap.astype(BF16)
-    for step in (1, 7, 2, 6, 3, 5, 4):
+    for step in (4, 3, 5, 2, 6, 1, 7):
         send(here, here, {"head": at_z(step)}, f"c{step}", "z")
+
+    target_ref[...] = ((context - mean) * scale).astype(BF16)
 
     def half_a(source, half):
         return abuf.at[source, pl.ds(half * CHANNELS, CHANNELS), :]
@@ -448,6 +453,7 @@
         rows = pl.ds(owner * CHANNELS, CHANNELS)
         return dot(cot[rows, :], downbuf[rows, :], ((0,), (0,)))
 
+    operand("nrm", 1, lambda to: normed_t.at[pl.ds(to * SHARD, SHARD), :], whole_a)
     pass_on(z)
     back = back_from(z)
     for step in (1, 7, 2, 6, 3, 5, 4):
@@ -658,7 +664,7 @@
             pltpu.SemaphoreType.DMA((RECEIVES,)),
         ],
         compiler_params=pltpu.CompilerParams(
-            collective_id=0, has_side_effects=True, vmem_limit_bytes=32 * 1024 * 1024
+            collective_id=0, has_side_effects=True, vmem_limit_bytes=60 * 1024 * 1024
         ),
     )(
         frames[0],

time: 103 us -> 96.4 us (0.936)
  local copies, waits for them, and re-layouts: 7.56 us -> 0 us
  Pallas kernels: 92.8 us -> 94.6 us
    unnamed x18 -> x0, local copies, waits for them, and re-layouts: 7.56 us -> none
    pallas_call x1, Pallas kernels: 90.4 us -> 92.2 us  [local(): pl.pallas_call(kernel, out_shape=(jax.ShapeDtypeStruct((CHANNELS, FRAMES)...]
where the time goes in v5:
time: 96.4 us; the launch traced here: 95.9 us
  Pallas kernels  94.6 us (98%)
  between operations  1.29 us (1%)
    pallas_call x1, Pallas kernels, local(): pl.pallas_call(kernel, out_shape=(jax.ShapeDtypeStruct((CHANNELS, FRAMES)...  92.2 us
    pallas_call x1, Pallas kernels, local(): pl.pallas_call(widen, out_shape=(jax.ShapeDtypeStruct((CHANNELS, FRAMES),...  2.4 us

profile of v5, /device:TPU:1, one launch (start us, length us, event | category | flops | bytes accessed | tf_op | source)
XLA Modules:
  0.0 95.9 jit_solution(14157592475378892224)
XLA Ops:
  1.3 92.2 %shard_map.94 = (bf16[160,256]{1,0:T(8,128)(2,1)}, bf16[320,640]{1,0:T(8,128)(2,1)}, bf16[320,640]{1,0:T(8,128)(2,1)}) custom-call(bf16[256,1280]{1,0:T(8,128)(2,1)} %bitcast.7, s32[1,256]{1,0:T(1,128)} %masked_ref.1, s32[1,1]{1,0:T(1,128)S(6)} %copy.10.counts_ref, f32[1280]{0:T(1024)} %gain_ref.1, bf16[480,320]{1,0:T(8,128)(2,1)} %bitcast.8, ...), custom_call_target="tpu_custom_call" | custom-call | tf_op jit(solution)/shard_map/pallas_call | solution.py:630
  93.5 2.4 %shard_map.95 = (bf16[160,256]{1,0:T(8,128)(2,1)}, f32[320,640]{1,0:T(8,128)}, f32[320,640]{1,0:T(8,128)}) custom-call(bf16[160,256]{1,0:T(8,128)(2,1)} %get-tuple-element.9.target_ref, bf16[320,640]{1,0:T(8,128)(2,1)} %get-tuple-element.10.gup_ref, bf16[320,640]{1,0:T(8,128)(2,1)} %get-tuple-element.11.gdown_ref), custom_call_target="tpu_custom_call" | custom-call | tf_op jit(solution)/shard_map/pallas_call | solution.py:678

commit v6 on v5

--- a/solution.py
+++ b/solution.py
@@ -44,15 +44,18 @@
 
 def kernel(
     frames_hbm,
-    masked_ref,
+    masked_hbm,
     counts_ref,
-    gain_ref,
+    gain_hbm,
     wt_ref,
     up_ref,
     down_ref,
+    target_hbm,
+    gup_hbm,
+    gdown_hbm,
     target_ref,
-    gup_ref,
-    gdown_ref,
+    masked_ref,
+    gain_ref,
     frames_ref,
     wbuf,
     upbuf,
@@ -95,8 +98,15 @@
     def at_z(step):
         return lax.rem(z + step + NZ, NZ)
 
-    fetch = pltpu.make_async_copy(frames_hbm, frames_ref, local_sem.at[4])
-    fetch.start()
+    own_w = pltpu.make_async_copy(wt_ref, wbuf.at[x], local_sem.at[0])
+    own_mask = pltpu.make_async_copy(masked_hbm, masked_ref, local_sem.at[1])
+    own_gain = pltpu.make_async_copy(gain_hbm, gain_ref, local_sem.at[2])
+    own_frames = pltpu.make_async_copy(frames_hbm, frames_ref, local_sem.at[3])
+    own_rows = pl.ds(x * SHARD, SHARD)
+    own_up = pltpu.make_async_copy(up_ref, upbuf.at[own_rows, :], local_sem.at[4])
+    own_down = pltpu.make_async_copy(down_ref, downbuf.at[own_rows, :], local_sem.at[5])
+    for copy in (own_w, own_mask, own_gain, own_frames, own_up, own_down):
+        copy.start()
 
     barrier = pltpu.get_barrier_semaphore()
     peers = [partner]
@@ -152,19 +162,14 @@
         return downbuf.at[pl.ds(shard * SHARD + row, rows), :]
 
     class Direct:
-        def __init__(self, name, src, place, base, half, sem):
-            self.name, self.src, self.place, self.half = name, src, place, half
+        def __init__(self, name, place, base, half):
+            self.name, self.place, self.half = name, place, half
             self.mine, self.theirs = base + c * half, base + other * half
-            self.own = pltpu.make_async_copy(
-                src.at[pl.ds(base, 2 * half), :], place(x, base, 2 * half), local_sem.at[sem]
-            )
 
         def start(self):
-            mine = self.src.at[pl.ds(self.mine, self.half), :]
-            there = self.place(x, self.mine, self.half)
+            mine = self.place(x, self.mine, self.half)
             for step in NEAR:
-                send(mine, there, {"dp": at_x(step)}, f"{self.name}{step}", "w")
-            self.own.start()
+                send(mine, mine, {"dp": at_x(step)}, f"{self.name}{step}", "w")
 
         def share(self):
             for step in NEAR:
@@ -173,22 +178,18 @@
                 send(block, block, partner, f"{self.name}P", "w")
 
         def finish(self):
-            self.own.wait()
             wait(wbuf.at[pl.ds(0, NX - 1), pl.ds(self.theirs, self.half), :], f"{self.name}P")
 
     class Relay:
-        def __init__(self, name, src, place, half, first, sem):
-            self.name, self.src, self.place = name, src, place
+        def __init__(self, name, place, half, first):
+            self.name, self.place = name, place
             self.half, self.first = half, first
             self.mine, self.theirs = c * half, other * half
-            self.own = pltpu.make_async_copy(src, place(x, 0, 2 * half), local_sem.at[sem])
 
         def start(self):
-            mine = self.src.at[pl.ds(self.mine, self.half), :]
-            there = self.place(x, self.mine, self.half)
-            send(mine, there, {"dp": at_x(1)}, self.name + "R0", self.name)
-            send(mine, there, {"dp": at_x(-1)}, self.name + "L0", self.name)
-            self.own.start()
+            mine = self.place(x, self.mine, self.half)
+            send(mine, mine, {"dp": at_x(1)}, self.name + "R0", self.name)
+            send(mine, mine, {"dp": at_x(-1)}, self.name + "L0", self.name)
 
         def relay(self):
             n, first = self.half, self.first
@@ -214,20 +215,21 @@
             send(part, part, partner, self.name + "P2", self.name)
 
         def near(self):
-            self.own.wait()
             wait(self.place(0, 0, 2 * self.half), self.name + "P0")
 
         def far(self):
             wait(self.place(at_x(2), self.theirs, self.half), self.name + "P2")
 
-    teacher_kv = Direct("w", wt_ref, place_w, CHANNELS, CHANNELS, 0)
-    teacher_q = Direct("q", wt_ref, place_w, 0, HEAD, 3)
-    upward = Relay("u", up_ref, place_up, 160, 80, 1)
-    downward = Relay("d", down_ref, place_down, 160, 80, 2)
-
+    teacher_kv = Direct("w", place_w, CHANNELS, CHANNELS)
+    teacher_q = Direct("q", place_w, 0, HEAD)
+    upward = Relay("u", place_up, 160, 80)
+    downward = Relay("d", place_down, 160, 80)
+
+    own_w.wait()
     teacher_kv.start()
     teacher_q.start()
 
+    own_mask.wait()
     keep = 1 - masked_ref[...]
     keep = keep.astype(F32)
     before = lax.broadcasted_iota(jnp.int32, (FRAMES, FRAMES), 0)
@@ -236,7 +238,8 @@
     rank = dot(jnp.broadcast_to(keep, (16, FRAMES)).astype(BF16), upper, ((1,), (0,)))[0:1]
     slot = lax.broadcasted_iota(jnp.int32, (SLOTS, FRAMES), 0).astype(F32)
     pick = jnp.where(rank - 1.0 == slot, jnp.broadcast_to(keep, (SLOTS, FRAMES)), 0.0).astype(BF16)
-    fetch.wait()
+    own_frames.wait()
+    own_gain.wait()
     chosen = dot(pick, frames_ref[...], ((1,), (0,)))
     centre = jnp.mean(chosen, axis=1, keepdims=True)
     chosen = chosen - centre
@@ -257,6 +260,8 @@
         return kv.at[source, core, pl.ds(part * CHANNELS, CHANNELS), :]
 
     teacher_kv.share()
+    own_up.wait()
+    own_down.wait()
     upward.start()
     downward.start()
     teacher_kv.finish()
@@ -430,6 +435,8 @@
         send(here, here, {"head": at_z(step)}, f"c{step}", "z")
 
     target_ref[...] = ((context - mean) * scale).astype(BF16)
+    target_out = pltpu.make_async_copy(target_ref, target_hbm, local_sem.at[6])
+    target_out.start()
 
     def half_a(source, half):
         return abuf.at[source, pl.ds(half * CHANNELS, CHANNELS), :]
@@ -582,22 +589,27 @@
     gather_first(1)
     gather_last(0)
     gather_last(1)
+    def results(number):
+        band, _, rows = CHUNKS[number]
+        part = pl.ds(band * SHARD, NY * rows)
+        pairs = ((gdown_hbm, gup_hbm), (gup_hbm, gdown_hbm))
+        return [
+            [
+                pltpu.make_async_copy(source.at[part, :], out.at[part, :], local_sem.at[7 + 2 * number + at])
+                for at, (source, out) in enumerate(zip((fown, foth), pair))
+            ]
+            for pair in pairs
+        ]
+
+    written = [results(number) for number in range(len(CHUNKS))]
     for number, (band, _, rows) in enumerate(CHUNKS):
         wait(foth.at[pl.ds(band * SHARD, NY * rows), :], f"h{number}")
-
-    def unstack(source, out):
-        for band in range(HIDDEN // 128):
-            out[:, band * 128 : (band + 1) * 128] = source[band * SHARD : (band + 1) * SHARD, :]
-
-    @pl.when(c == 0)
-    def _():
-        unstack(fown, gdown_ref)
-        unstack(foth, gup_ref)
-
-    @pl.when(c != 0)
-    def _():
-        unstack(fown, gup_ref)
-        unstack(foth, gdown_ref)
+        for core in range(2):
+
+            @pl.when(c == core)
+            def _():
+                for copy in written[number][core]:
+                    copy.start()
 
     wait_left("w", wbuf.at[pl.ds(0, NX - 1)])
     wait_left("p", pieces((NZ - 1) * CHANNELS))
@@ -614,13 +626,41 @@
         wait_left("partner", pieces(left_here["partner1"]))
         wait_left("e", pieces(NZ * CHANNELS))
 
+    target_out.wait()
+    for core in range(2):
+
+        @pl.when(c == core)
+        def _():
+            for number in range(len(CHUNKS)):
+                for copy in written[number][core]:
+                    copy.wait()
+
     assert len(names.index) <= RECEIVES and len(outs.index) <= SENDS
 
 
-def widen(target_ref, gup_ref, gdown_ref, target_out, gup_out, gdown_out):
-    target_out[...] = target_ref[...]
-    gup_out[...] = gup_ref[...].astype(F32)
-    gdown_out[...] = gdown_ref[...].astype(F32)
+def widen(target_in, gup_in, gdown_in, target_out, gup_out, gdown_out, narrow, wide, sems):
+    through = pltpu.make_async_copy(target_in, target_out, sems.at[8])
+    pieces = []
+    for at, (source, out) in enumerate(((gup_in, gup_out), (gdown_in, gdown_out))):
+        for half, (band, bands) in enumerate(((0, 3), (3, 2))):
+            rows, columns = pl.ds(band * SHARD, bands * SHARD), pl.ds(band * 128, bands * 128)
+            here, sem = wide.at[at, :, columns], 2 * at + half
+            come = pltpu.make_async_copy(source.at[rows, :], narrow.at[at, rows, :], sems.at[sem])
+            go = pltpu.make_async_copy(here, out.at[:, columns], sems.at[4 + sem])
+            pieces.append((at, band, bands, come, go))
+    for *_, come, _ in pieces:
+        come.start()
+    through.start()
+    for at, band, bands, come, go in pieces:
+        come.wait()
+        for number in range(band, band + bands):
+            wide[at, :, number * 128 : (number + 1) * 128] = narrow[
+                at, number * SHARD : (number + 1) * SHARD, :
+            ].astype(F32)
+        go.start()
+    for *_, go in pieces:
+        go.wait()
+    through.wait()
 
 
 def local(frames, masked, kept_counts, teacher_qkv, student_gain, w_up, w_down):
@@ -631,12 +671,15 @@
         kernel,
         out_shape=(
             jax.ShapeDtypeStruct((CHANNELS, FRAMES), BF16),
-            jax.ShapeDtypeStruct((SHARD, HIDDEN), BF16),
-            jax.ShapeDtypeStruct((SHARD, HIDDEN), BF16),
+            jax.ShapeDtypeStruct((STACK, 128), BF16),
+            jax.ShapeDtypeStruct((STACK, 128), BF16),
         ),
-        in_specs=[hbm, vmem, vmem, vmem, hbm, hbm, hbm],
-        out_specs=(vmem, vmem, vmem),
+        in_specs=[hbm, hbm, vmem, hbm, hbm, hbm, hbm],
+        out_specs=(hbm, hbm, hbm),
         scratch_shapes=[
+            pltpu.VMEM((CHANNELS, FRAMES), BF16),
+            pltpu.VMEM((1, FRAMES), jnp.int32),
+            pltpu.VMEM((D,), F32),
             pltpu.VMEM((FRAMES, D), BF16),
             pltpu.VMEM((NX, 3 * CHANNELS, SHARD), BF16),
             pltpu.VMEM((D, HIDDEN), BF16),
@@ -659,7 +702,7 @@
             pltpu.VMEM((STACK, 128), BF16),
             pltpu.VMEM((STACK, 128), BF16),
             pltpu.VMEM((METER, 128), BF16),
-            pltpu.SemaphoreType.DMA((5,)),
+            pltpu.SemaphoreType.DMA((11,)),
             pltpu.SemaphoreType.DMA((SENDS,)),
             pltpu.SemaphoreType.DMA((RECEIVES,)),
         ],
@@ -682,8 +725,14 @@
             jax.ShapeDtypeStruct((SHARD, HIDDEN), F32),
             jax.ShapeDtypeStruct((SHARD, HIDDEN), F32),
         ),
-        in_specs=[vmem] * 3,
-        out_specs=(vmem, vmem, vmem),
+        in_specs=[hbm] * 3,
+        out_specs=(hbm, hbm, hbm),
+        scratch_shapes=[
+            pltpu.VMEM((2, STACK, 128), BF16),
+            pltpu.VMEM((2, SHARD, HIDDEN), F32),
+            pltpu.SemaphoreType.DMA((9,)),
+        ],
+        compiler_params=pltpu.CompilerParams(vmem_limit_bytes=60 * 1024 * 1024),
     )(target, gup, gdown)
     return target.T[None], gup, gdown
 

time: 96.4 us -> 96.2 us (level)
    pallas_call x1, Pallas kernels: 92.2 us -> 90.7 us  [local(): pl.pallas_call(kernel, out_shape=(jax.ShapeDtypeStruct((CHANNELS, FRAMES)...]
    pallas_call x1, Pallas kernels: 2.4 us -> 3.67 us  [local(): pl.pallas_call(widen, out_shape=(jax.ShapeDtypeStruct((CHANNELS, FRAMES),...]
where the time goes in v6:
time: 96.2 us; the launch traced here: 95.7 us
  Pallas kernels  94.4 us (98%)
  between operations  1.29 us (1%)
    pallas_call x1, Pallas kernels, local(): pl.pallas_call(kernel, out_shape=(jax.ShapeDtypeStruct((CHANNELS, FRAMES)...  90.7 us
    pallas_call x1, Pallas kernels, local(): pl.pallas_call(widen, out_shape=(jax.ShapeDtypeStruct((CHANNELS, FRAMES),...  3.67 us

profile of v6, /device:TPU:1, one launch (start us, length us, event | category | flops | bytes accessed | tf_op | source)
XLA Modules:
  0.0 95.7 jit_solution(10509535627652488048)
XLA Ops:
  1.3 90.7 %shard_map.94 = (bf16[160,256]{1,0:T(8,128)(2,1)}, bf16[1664,128]{1,0:T(8,128)(2,1)}, bf16[1664,128]{1,0:T(8,128)(2,1)}) custom-call(bf16[256,1280]{1,0:T(8,128)(2,1)} %bitcast.7, s32[1,256]{1,0:T(1,128)} %masked_hbm.1, s32[1,1]{1,0:T(1,128)S(6)} %copy.10.counts_ref, f32[1280]{0:T(1024)} %gain_hbm.1, bf16[480,320]{1,0:T(8,128)(2,1)} %bitcast.8, ...), custom_call_target="tpu_custom_call" | custom-call | tf_op jit(solution)/shard_map/pallas_call | solution.py:670
  92.0 3.7 %shard_map.95 = (bf16[160,256]{1,0:T(8,128)(2,1)}, f32[320,640]{1,0:T(8,128)}, f32[320,640]{1,0:T(8,128)}) custom-call(bf16[160,256]{1,0:T(8,128)(2,1)} %get-tuple-element.9.target_in, bf16[1664,128]{1,0:T(8,128)(2,1)} %get-tuple-element.10.gup_in, bf16[1664,128]{1,0:T(8,128)(2,1)} %get-tuple-element.11.gdown_in), custom_call_target="tpu_custom_call" | custom-call | tf_op jit(solution)/shard_map/pallas_call | solution.py:721

commit v7 on v6

--- a/solution.py
+++ b/solution.py
@@ -638,29 +638,33 @@
     assert len(names.index) <= RECEIVES and len(outs.index) <= SENDS
 
 
-def widen(target_in, gup_in, gdown_in, target_out, gup_out, gdown_out, narrow, wide, sems):
-    through = pltpu.make_async_copy(target_in, target_out, sems.at[8])
-    pieces = []
-    for at, (source, out) in enumerate(((gup_in, gup_out), (gdown_in, gdown_out))):
-        for half, (band, bands) in enumerate(((0, 3), (3, 2))):
-            rows, columns = pl.ds(band * SHARD, bands * SHARD), pl.ds(band * 128, bands * 128)
-            here, sem = wide.at[at, :, columns], 2 * at + half
-            come = pltpu.make_async_copy(source.at[rows, :], narrow.at[at, rows, :], sems.at[sem])
-            go = pltpu.make_async_copy(here, out.at[:, columns], sems.at[4 + sem])
-            pieces.append((at, band, bands, come, go))
-    for *_, come, _ in pieces:
+def widen(target_in, gup_in, gdown_in, target_out, gup_out, gdown_out, target, narrow, wide, sems):
+    target_come = pltpu.make_async_copy(target_in, target, sems.at[0])
+    target_go = pltpu.make_async_copy(target, target_out, sems.at[1])
+    comes = [
+        pltpu.make_async_copy(source, narrow.at[at], sems.at[2 + at])
+        for at, source in enumerate((gup_in, gdown_in))
+    ]
+    for come in comes:
         come.start()
-    through.start()
-    for at, band, bands, come, go in pieces:
-        come.wait()
-        for number in range(band, band + bands):
-            wide[at, :, number * 128 : (number + 1) * 128] = narrow[
-                at, number * SHARD : (number + 1) * SHARD, :
-            ].astype(F32)
-        go.start()
-    for *_, go in pieces:
+    target_come.start()
+    goes = []
+    for at, out in enumerate((gup_out, gdown_out)):
+        comes[at].wait()
+        for half in range(2):
+            low, rows = half * CHANNELS, pl.ds(half * CHANNELS, CHANNELS)
+            for band in range(HIDDEN // 128):
+                source = narrow[at, band * SHARD + low : band * SHARD + low + CHANNELS, :]
+                wide[at, low : low + CHANNELS, band * 128 : (band + 1) * 128] = source.astype(F32)
+            goes.append(
+                pltpu.make_async_copy(wide.at[at, rows, :], out.at[rows, :], sems.at[4 + 2 * at + half])
+            )
+            goes[-1].start()
+    target_come.wait()
+    target_go.start()
+    for go in goes:
         go.wait()
-    through.wait()
+    target_go.wait()
 
 
 def local(frames, masked, kept_counts, teacher_qkv, student_gain, w_up, w_down):
@@ -728,9 +732,10 @@
         in_specs=[hbm] * 3,
         out_specs=(hbm, hbm, hbm),
         scratch_shapes=[
+            pltpu.VMEM((CHANNELS, FRAMES), BF16),
             pltpu.VMEM((2, STACK, 128), BF16),
             pltpu.VMEM((2, SHARD, HIDDEN), F32),
-            pltpu.SemaphoreType.DMA((9,)),
+            pltpu.SemaphoreType.DMA((8,)),
         ],
         compiler_params=pltpu.CompilerParams(vmem_limit_bytes=60 * 1024 * 1024),
     )(target, gup, gdown)

time: 96.2 us -> 94.8 us (0.985)
  Pallas kernels: 94.4 us -> 93 us
    pallas_call x1, Pallas kernels: 3.67 us -> 2.28 us  [local(): pl.pallas_call(widen, out_shape=(jax.ShapeDtypeStruct((CHANNELS, FRAMES),...]
where the time goes in v7:
time: 94.8 us; the launch traced here: 94.3 us
  Pallas kernels  93 us (98%)
  between operations  1.29 us (1%)
    pallas_call x1, Pallas kernels, local(): pl.pallas_call(kernel, out_shape=(jax.ShapeDtypeStruct((CHANNELS, FRAMES)...  90.7 us
    pallas_call x1, Pallas kernels, local(): pl.pallas_call(widen, out_shape=(jax.ShapeDtypeStruct((CHANNELS, FRAMES),...  2.28 us

profile of v7, /device:TPU:1, one launch (start us, length us, event | category | flops | bytes accessed | tf_op | source)
XLA Modules:
  0.0 94.3 jit_solution(4073902615701678086)
XLA Ops:
  1.3 90.7 %shard_map.94 = (bf16[160,256]{1,0:T(8,128)(2,1)}, bf16[1664,128]{1,0:T(8,128)(2,1)}, bf16[1664,128]{1,0:T(8,128)(2,1)}) custom-call(bf16[256,1280]{1,0:T(8,128)(2,1)} %bitcast.7, s32[1,256]{1,0:T(1,128)} %masked_hbm.1, s32[1,1]{1,0:T(1,128)S(6)} %copy.10.counts_ref, f32[1280]{0:T(1024)} %gain_hbm.1, bf16[480,320]{1,0:T(8,128)(2,1)} %bitcast.8, ...), custom_call_target="tpu_custom_call" | custom-call | tf_op jit(solution)/shard_map/pallas_call | solution.py:674
  92.0 2.3 %shard_map.95 = (bf16[160,256]{1,0:T(8,128)(2,1)}, f32[320,640]{1,0:T(8,128)}, f32[320,640]{1,0:T(8,128)}) custom-call(bf16[160,256]{1,0:T(8,128)(2,1)} %get-tuple-element.9.target_in, bf16[1664,128]{1,0:T(8,128)(2,1)} %get-tuple-element.10.gup_in, bf16[1664,128]{1,0:T(8,128)(2,1)} %get-tuple-element.11.gdown_in), custom_call_target="tpu_custom_call" | custom-call | tf_op jit(solution)/shard_map/pallas_call | solution.py:725

commit v8 on v7

--- a/solution.py
+++ b/solution.py
@@ -400,7 +400,7 @@
         columns = jnp.where(lane == h, first, jnp.where(lane == 2 + h, second, columns))
     columns = jnp.concatenate([columns, jnp.zeros((128 - HEAD, 128), F32)], axis=0)
     stats[0] = columns.T[0:8]
-    for step in range(1, NT):
+    for step in (8, 7, 9, 6, 10, 5, 11, 4, 12, 3, 13, 2, 14, 15, 1):
         send(stats.at[0], stats.at[step], {"tm": lax.rem(t + step, NT)}, "stats", "z")
 
 

time: 94.8 us -> 94.8 us (level); the launches traced: 94.3 us -> 93.2 us
  Pallas kernels: 93 us -> 91.9 us
    pallas_call x1, Pallas kernels: 90.7 us -> 89.6 us  [local(): pl.pallas_call(kernel, out_shape=(jax.ShapeDtypeStruct((CHANNELS, FRAMES)...]
where the time goes in v8:
time: 94.8 us; the launch traced here: 93.2 us
  Pallas kernels  91.9 us (97%)
  between operations  1.29 us (1%)
    pallas_call x1, Pallas kernels, local(): pl.pallas_call(kernel, out_shape=(jax.ShapeDtypeStruct((CHANNELS, FRAMES)...  89.6 us
    pallas_call x1, Pallas kernels, local(): pl.pallas_call(widen, out_shape=(jax.ShapeDtypeStruct((CHANNELS, FRAMES),...  2.28 us

profile of v8, /device:TPU:1, one launch (start us, length us, event | category | flops | bytes accessed | tf_op | source)
XLA Modules:
  0.0 93.2 jit_solution(16203771276257353693)
XLA Ops:
  1.3 89.6 %shard_map.94 = (bf16[160,256]{1,0:T(8,128)(2,1)}, bf16[1664,128]{1,0:T(8,128)(2,1)}, bf16[1664,128]{1,0:T(8,128)(2,1)}) custom-call(bf16[256,1280]{1,0:T(8,128)(2,1)} %bitcast.7, s32[1,256]{1,0:T(1,128)} %masked_hbm.1, s32[1,1]{1,0:T(1,128)S(6)} %copy.10.counts_ref, f32[1280]{0:T(1024)} %gain_hbm.1, bf16[480,320]{1,0:T(8,128)(2,1)} %bitcast.8, ...), custom_call_target="tpu_custom_call" | custom-call | tf_op jit(solution)/shard_map/pallas_call | solution.py:674
  90.9 2.3 %shard_map.95 = (bf16[160,256]{1,0:T(8,128)(2,1)}, f32[320,640]{1,0:T(8,128)}, f32[320,640]{1,0:T(8,128)}) custom-call(bf16[160,256]{1,0:T(8,128)(2,1)} %get-tuple-element.9.target_in, bf16[1664,128]{1,0:T(8,128)(2,1)} %get-tuple-element.10.gup_in, bf16[1664,128]{1,0:T(8,128)(2,1)} %get-tuple-element.11.gdown_in), custom_call_target="tpu_custom_call" | custom-call | tf_op jit(solution)/shard_map/pallas_call | solution.py:725
